TPU v7x, 512 devices: a whole 4x8x8 slice. The times are simulated.
512 devices in a mesh: dp: 8 (over x, core), view: 64 (over y, z).
Axes of the slice: x: 4, y: 8, z: 8, core: 2. Of those that a mesh axis runs over, the one named last changes fastest.
Arguments:
- queries: bfloat16 [8, 8192, 2048], P('dp', 'view')
- keys: bfloat16 [8, 8192, 2048], P('dp', 'view')
- values: bfloat16 [8, 8192, 2048], P('dp', 'view'), may hold values from -6 to 6
- out_grad: bfloat16 [8, 8192, 2048], P('dp', 'view'), may hold values from -6 to 6
- gain: float32 [16, 128], replicated, may hold values from 0.1 to 1.9
- tasks: int32 [8, 64, 2], P('dp', 'view'), may hold values 0 or 1
- bounds: int32 [8, 64, 2], P('dp', 'view'), may hold values from 0 to 128, as said below
Outputs:
- attended: bfloat16 [8, 8192, 2048], P('dp', 'view')
- query_grad: bfloat16 [8, 8192, 2048], P('dp', 'view')
- key_grad: bfloat16 [8, 8192, 2048], P('dp', 'view')
- value_grad: bfloat16 [8, 8192, 2048], P('dp', 'view')
- gain_grad: float32 [16, 128], replicated
Inputs may be any that keep to these rules, and one draw needn't show every extreme that they name: bounds[.,.,0] lies in 0 to 31 and bounds[.,.,1] in 97 to 128.
All inputs are finite; a program needn't handle non-finite values. No bound on the sum of `tasks` on one device may be relied on, other than what follows from the above.
Results may differ from a plain program's by a relative error of at most 0.003.
The roundings to bfloat16 on the way count: a program that leaves them out, or rounds other values in their place, can miss the bound.
Values may be sent and summed in bfloat16 or wider, within the bound.
No kernel may reach another device: no remote copies, remote signals or barrier semaphores. Data moves between devices by JAX's collectives and lax.ppermute only.
A program may use at most 64 MiB of HBM per device.

v0:
```python
import jax
import jax.numpy as jnp
from jax import lax
from jax.sharding import PartitionSpec as P

HEADS = 16
HEAD_DIM = 128


OFFSETS = (-1, 1)


def shifted(array, axis, by):
    count = lax.axis_size(axis)
    return lax.ppermute(array, axis, [(i, (i + by) % count) for i in range(count)])


def on_device(queries, keys, values, out_grad, gain, tasks, bounds):
    strip = queries.shape[1]
    shape = (strip, HEADS, HEAD_DIM)
    inv = 1.0 / jnp.sqrt(jnp.float32(HEAD_DIM))
    q_full = queries[0].reshape(shape).astype(jnp.float32)
    scale_r = lax.rsqrt(jnp.mean(q_full * q_full, axis=-1) + 1e-06)
    normed = (q_full * scale_r[..., None] * gain).astype(jnp.bfloat16)
    keys_own = keys[0].reshape(shape)
    values_own = values[0].reshape(shape)
    dout = out_grad[0].reshape(shape)
    rows = jnp.arange(strip, dtype=jnp.int32)
    own_valid = (rows >= bounds[0, 0, 0]) & (rows < bounds[0, 0, 1])
    valid_flag = own_valid.astype(jnp.bfloat16)
    key_list = [keys_own]
    value_list = [values_own]
    live_list = [own_valid]
    for idx, offset in enumerate(OFFSETS):
        far_k, far_v, far_valid = shifted((keys_own, values_own, valid_flag), "view", -offset)
        key_list.append(far_k)
        value_list.append(far_v)
        live_list.append((far_valid > 0) & (tasks[0, 0, idx] > 0))
    keys_all = jnp.concatenate(key_list, axis=0)
    values_all = jnp.concatenate(value_list, axis=0)
    live = jnp.concatenate(live_list, axis=0)
    scores = jnp.einsum("qhd,khd->hqk", normed, keys_all, preferred_element_type=jnp.float32) * inv
    scores = jnp.where(live[None, None, :], scores, jnp.float32(-1e30))
    rowmax = jnp.max(scores, axis=-1)
    expo = jnp.exp(scores - rowmax[..., None])
    total = jnp.sum(expo, axis=-1)
    prob = expo / total[..., None]
    prob_b = prob.astype(jnp.bfloat16)
    attended = jnp.einsum(
        "hqk,khd->qhd", prob_b, values_all, preferred_element_type=jnp.float32
    ).astype(jnp.bfloat16)
    dprob = jnp.einsum("qhd,khd->hqk", dout, values_all, preferred_element_type=jnp.float32)
    delta = jnp.sum(prob * dprob, axis=-1)
    dscore = (prob * (dprob - delta[..., None])).astype(jnp.bfloat16)
    dnormed = jnp.einsum("hqk,khd->qhd", dscore, keys_all, preferred_element_type=jnp.float32) * inv
    inner = jnp.sum(q_full * gain * dnormed, axis=-1)
    cubed = scale_r * scale_r * scale_r
    qgrad = gain * scale_r[..., None] * dnormed - q_full * (cubed * inner / HEAD_DIM)[..., None]
    gain_part = jnp.sum(q_full * scale_r[..., None] * dnormed, axis=0)
    kgrad = jnp.einsum("hqk,qhd->khd", dscore, normed, preferred_element_type=jnp.float32) * inv
    vgrad = jnp.einsum("hqk,qhd->khd", prob_b, dout, preferred_element_type=jnp.float32)
    ktotal = kgrad[:strip]
    vtotal = vgrad[:strip]
    for idx, offset in enumerate(OFFSETS):
        low = (idx + 1) * strip
        back_k, back_v = shifted(
            (kgrad[low : low + strip], vgrad[low : low + strip]), "view", offset
        )
        ktotal = ktotal + back_k
        vtotal = vtotal + back_v
    gain_grad = lax.psum(gain_part, ("dp", "view"))
    flat = (1, strip, HEADS * HEAD_DIM)
    return (
        attended.reshape(flat),
        qgrad.astype(jnp.bfloat16).reshape(flat),
        ktotal.astype(jnp.bfloat16).reshape(flat),
        vtotal.astype(jnp.bfloat16).reshape(flat),
        gain_grad,
    )


def solution(mesh):
    in_specs = (
        P("dp", "view", None),
        P("dp", "view", None),
        P("dp", "view", None),
        P("dp", "view", None),
        P(),
        P("dp", "view", None),
        P("dp", "view", None),
    )
    out_specs = (
        P("dp", "view", None),
        P("dp", "view", None),
        P("dp", "view", None),
        P("dp", "view", None),
        P(),
    )
    return jax.shard_map(
        on_device, mesh=mesh, in_specs=in_specs, out_specs=out_specs, check_vma=False
    )
```

profile of v0, /device:TPU:1, one launch (start us, length us, event | category | flops | bytes accessed | tf_op | source)
XLA Modules:
  0.0 216.4 jit_solution(7645244670405198291)
XLA Ops:
  0.7 1.3 fusion.29
  3.3 14.4 %collective-permute-start.3 = (bf16[128]{0:T(256)(128)(2,1)S(1)}, bf16[128]{0:T(256)(128)(2,1)S(1)}, u32[]{:S(2)}, u32[]{:S(2)}) collective-permute-start(bf16[128]{0:T(256)(128)(2,1)S(1)} %get-tuple-element.17), channel_id=1, source_target_pairs={{0,63},{1,0},{2,1},{3,2},{4,3},{5,4},{6,5},{7,6},{8,7},{9,8},{10,9... | collective-permute-start | bytes 776 | tf_op jit(solution)/shard_map/ppermute | solution.py:15
  17.7 1.9 collective-permute-start.2
  19.6 1.3 copy.24
  21.0 6.7 %collective-permute-start.1 = (bf16[128,16,128]{0,2,1:T(8,128)(2,1)S(1)}, bf16[128,16,128]{0,2,1:T(8,128)(2,1)}, u32[]{:S(2)}, u32[]{:S(2)}) collective-permute-start(bf16[128,16,128]{0,2,1:T(8,128)(2,1)S(1)} %bitcast.42), channel_id=1, source_target_pairs={{0,63},{1,0},{2,1},{3,2},{4,3},{5,4},{6,5},{7,6},{8,7},{9,8},{10,9... | collective-permute-start | bytes 1572872 | tf_op jit(solution)/shard_map/ppermute | solution.py:15
  27.7 1.9 collective-permute-start
  31.2 6.7 %collective-permute-start.5 = (bf16[128,16,128]{2,0,1:T(8,128)(2,1)S(1)}, bf16[128,16,128]{2,0,1:T(8,128)(2,1)}, u32[]{:S(2)}, u32[]{:S(2)}) collective-permute-start(bf16[128,16,128]{2,0,1:T(8,128)(2,1)S(1)} %copy.29), channel_id=1, source_target_pairs={{0,63},{1,0},{2,1},{3,2},{4,3},{5,4},{6,5},{7,6},{8,7},{9,8},{10,9... | collective-permute-start | bytes 1572872 | tf_op jit(solution)/shard_map/ppermute | solution.py:15
  40.4 1.9 collective-permute-start.4
  42.4 6.9 %collective-permute-done.5 = bf16[128,16,128]{2,0,1:T(8,128)(2,1)} collective-permute-done((bf16[128,16,128]{2,0,1:T(8,128)(2,1)S(1)}, bf16[128,16,128]{2,0,1:T(8,128)(2,1)}, u32[]{:S(2)}, u32[]{:S(2)}) %collective-permute-start.5) | collective-permute-done | bytes 524320 | tf_op jit(solution)/shard_map/ppermute | solution.py:15
  49.3 7.6 %collective-permute-done.4 = bf16[128,16,128]{2,0,1:T(8,128)(2,1)S(1)} collective-permute-done((bf16[128,16,128]{2,0,1:T(8,128)(2,1)S(1)}, bf16[128,16,128]{2,0,1:T(8,128)(2,1)S(1)}, u32[]{:S(2)}, u32[]{:S(2)}) %collective-permute-start.4) | collective-permute-done | bytes 524320 | tf_op jit(solution)/shard_map/ppermute | solution.py:15
  57.0 2.3 %fusion.15 = f32[16,128,384]{2,1,0:T(8,128)S(1)} fusion(bf16[128,16,128]{2,0,1:T(8,128)(2,1)} %collective-permute-done.5, bf16[128,16,128]{2,0,1:T(8,128)(2,1)S(1)} %collective-permute-done.4, bf16[128,16,128]{2,0,1:T(8,128)(2,1)S(1)} %copy.29, f32[128,16,128]{0,2,1:T(8,128)S(1)} %bitcast.34, f32[16,128]{1,0:T(8,128)S(1)} %copy-done.8, ...), kind=kOutput, calls=%fused_computation.33 | convolution fusion | flops 206831616 | bytes 5783552 | tf_op jit(solution)/shard_map/qhd,khd->hqk/dot_general | solution.py:42
  60.5 2.9 %convolution_convert_fusion = bf16[16,128,128]{2,1,0:T(8,128)(2,1)S(1)} fusion(bf16[128,16,128]{0,2,1:T(8,128)(2,1)} %collective-permute-done.1, bf16[128,16,128]{0,2,1:T(8,128)(2,1)} %collective-permute-done, bf16[128,16,128]{0,2,1:T(8,128)(2,1)S(1)} %bitcast.44, f32[16,128,384]{2,1,0:T(8,128)S(1)} %get-tuple-element.28, f32[16,128]{1,0:T(8,128)S(1)} %get-tuple-element.27), kind=kOutput, calls=%fused_computation.19 | convolution fusion | flops 207880192 | bytes 5251072 | tf_op jit(solution)/shard_map/hqk,khd->qhd/dot_general | solution.py:49
  64.4 2.7 %convolution_bitcast_fusion = f32[384,16,128]{0,2,1:T(8,128)S(1)} fusion(bf16[128,16,128]{0,2,1:T(8,128)(2,1)S(1)} %bitcast.46, f32[16,128,384]{2,1,0:T(8,128)} %copy-done.2, f32[16,128]{1,0:T(8,128)S(1)} %get-tuple-element.27), kind=kOutput, calls=%fused_computation.10 | convolution fusion | flops 202899456 | bytes 6823936 | tf_op jit(solution)/shard_map/hqk,qhd->khd/dot_general | solution.py:61
  67.2 2.5 %fusion.1 = (f32[16,128]{1,0:T(8,128)S(1)}, f32[16,384,128]{1,2,0:T(8,128)S(1)}) fusion(f32[16,128,384]{2,1,0:T(8,128)S(1)} %copy-done.3, f32[16,128]{1,0:T(8,128)S(1)} %get-tuple-element.27, bf16[128,16,128]{0,2,1:T(8,128)(2,1)S(1)} %bitcast.47, bf16[128,16,128]{0,2,1:T(8,128)(2,1)} %collective-permute-done.1, ...), kind=kOutput, calls=%fused_computation.3 | convolution fusion | flops 208402432 | bytes 8404992 | tf_op jit(solution)/shard_map/qhd,khd->hqk/dot_general | solution.py:52
  71.1 1.8 fusion.27
  73.0 2.0 collective-permute-start.6
  75.0 3.4 %collective-permute-start.7 = (f32[128,16,128]{0,2,1:T(8,128)}, f32[128,16,128]{0,2,1:T(8,128)}, u32[]{:S(2)}, u32[]{:S(2)}) collective-permute-start(f32[128,16,128]{0,2,1:T(8,128)} %get-tuple-element.22), channel_id=1, source_target_pairs={{0,1},{1,2},{2,3},{3,4},{4,5},{5,6},{6,7},{7,8},{8,9},{9,10},{10,1... | collective-permute-start | bytes 3145736 | tf_op jit(solution)/shard_map/ppermute | solution.py:15
  78.4 1.6 fusion.26
  80.0 5.2 %collective-permute-start.8 = (f32[128,16,128]{0,2,1:T(8,128)}, f32[128,16,128]{0,2,1:T(8,128)S(1)}, u32[]{:S(2)}, u32[]{:S(2)}) collective-permute-start(f32[128,16,128]{0,2,1:T(8,128)} %get-tuple-element.19), channel_id=1, source_target_pairs={{0,63},{1,0},{2,1},{3,2},{4,3},{5,4},{6,5},{7,6},{8,7},{9,8},{10,9... | collective-permute-start | bytes 3145736 | tf_op jit(solution)/shard_map/ppermute | solution.py:15
  85.2 1.9 collective-permute-start.9
  87.2 2.3 %multiply_reduce_fusion = (f32[16,128]{1,0:T(8,128)S(1)}, f32[128,16]{0,1:T(8,128)S(1)}, f32[128,16,128]{0,2,1:T(8,128)S(1)}) fusion(f32[128,16,128]{0,2,1:T(8,128)S(1)} %bitcast.36, f32[128,16]{0,1:T(8,128)S(1)} %add_rsqrt_fusion, f32[16,128]{1,0:T(8,128)S(1)} %copy-done.8, bf16[16,128,384]{2,1,0:T(8,128)(2,1)S(1)} %fusion.3, ...), kind=kOutput, calls=%fused_computation.26 | convolution fusion | flops 207876096 | bytes 5275648 | tf_op jit(solution)/shard_map/hqk,khd->qhd/dot_general | solution.py:55
  90.8 119.8 %psum.7 = f32[16,128]{1,0:T(8,128)} all-reduce(f32[16,128]{1,0:T(8,128)S(1)} %get-tuple-element.15), channel_id=1, replica_groups=mesh['dp'=8,'view'=64] {'dp','view'}, use_global_device_ids=true, to_apply=%region_6.7 | all-reduce | flops 2048 | bytes 16384 | tf_op jit(solution)/shard_map/psum | solution.py:71
  210.6 2.0 fusion.12
  213.7 1.7 fusion.10
  (48 shorter events, 11.2 us)
Async XLA Ops:
  0.6 37.3 %copy-start.9 = (s32[1,1,2]{2,1,0:T(1,128)S(1)}, s32[1,1,2]{2,1,0:T(1,128)}, u32[]{:S(2)}) copy-start(s32[1,1,2]{2,1,0:T(1,128)} %param.12) | copy-start | bytes 28
  0.6 37.8 %copy-start.4 = (bf16[1,128,2048]{2,1,0:T(8,128)(2,1)S(1)}, bf16[1,128,2048]{2,1,0:T(8,128)(2,1)}, u32[]{:S(2)}) copy-start(bf16[1,128,2048]{2,1,0:T(8,128)(2,1)} %param.7) | copy-start | bytes 1572868
  0.7 39.5 %copy-start.5 = (bf16[1,128,2048]{2,1,0:T(8,128)(2,1)S(1)}, bf16[1,128,2048]{2,1,0:T(8,128)(2,1)}, u32[]{:S(2)}) copy-start(bf16[1,128,2048]{2,1,0:T(8,128)(2,1)} %param.10) | copy-start | bytes 1572868
  3.3 37.1 %collective-permute-start.3 = (bf16[128]{0:T(256)(128)(2,1)S(1)}, bf16[128]{0:T(256)(128)(2,1)S(1)}, u32[]{:S(2)}, u32[]{:S(2)}) collective-permute-start(bf16[128]{0:T(256)(128)(2,1)S(1)} %get-tuple-element.17), channel_id=1, source_target_pairs={{0,63},{1,0},{2,1},{3,2},{4,3},{5,4},{6,5},{7,6},{8,7},{9,8},{10,9... | collective-permute-start | bytes 776 | tf_op jit(solution)/shard_map/ppermute | solution.py:15
  17.7 24.6 %collective-permute-start.2 = (bf16[128]{0:T(256)(128)(2,1)S(1)}, bf16[128]{0:T(256)(128)(2,1)S(1)}, u32[]{:S(2)}, u32[]{:S(2)}) collective-permute-start(bf16[128]{0:T(256)(128)(2,1)S(1)} %get-tuple-element.17), channel_id=1, source_target_pairs={{0,1},{1,2},{2,3},{3,4},{4,5},{5,6},{6,7},{7,8},{8,9},{9,10},{10,1... | collective-permute-start | bytes 776 | tf_op jit(solution)/shard_map/ppermute | solution.py:15
  21.0 36.0 %copy-start.8 = (f32[16,128]{1,0:T(8,128)S(1)}, f32[16,128]{1,0:T(8,128)}, u32[]{:S(2)}) copy-start(f32[16,128]{1,0:T(8,128)} %param.11) | copy-start | bytes 24580
  21.0 39.5 %collective-permute-start.1 = (bf16[128,16,128]{0,2,1:T(8,128)(2,1)S(1)}, bf16[128,16,128]{0,2,1:T(8,128)(2,1)}, u32[]{:S(2)}, u32[]{:S(2)}) collective-permute-start(bf16[128,16,128]{0,2,1:T(8,128)(2,1)S(1)} %bitcast.42), channel_id=1, source_target_pairs={{0,63},{1,0},{2,1},{3,2},{4,3},{5,4},{6,5},{7,6},{8,7},{9,8},{10,9... | collective-permute-start | bytes 1572872 | tf_op jit(solution)/shard_map/ppermute | solution.py:15
  27.7 32.8 %collective-permute-start = (bf16[128,16,128]{0,2,1:T(8,128)(2,1)S(1)}, bf16[128,16,128]{0,2,1:T(8,128)(2,1)}, u32[]{:S(2)}, u32[]{:S(2)}) collective-permute-start(bf16[128,16,128]{0,2,1:T(8,128)(2,1)S(1)} %bitcast.43), channel_id=1, source_target_pairs={{0,1},{1,2},{2,3},{3,4},{4,5},{5,6},{6,7},{7,8},{8,9},{9,10},{10,1... | collective-permute-start | bytes 1572872 | tf_op jit(solution)/shard_map/ppermute | solution.py:15
  31.2 18.1 %collective-permute-start.5 = (bf16[128,16,128]{2,0,1:T(8,128)(2,1)S(1)}, bf16[128,16,128]{2,0,1:T(8,128)(2,1)}, u32[]{:S(2)}, u32[]{:S(2)}) collective-permute-start(bf16[128,16,128]{2,0,1:T(8,128)(2,1)S(1)} %copy.29), channel_id=1, source_target_pairs={{0,63},{1,0},{2,1},{3,2},{4,3},{5,4},{6,5},{7,6},{8,7},{9,8},{10,9... | collective-permute-start | bytes 1572872 | tf_op jit(solution)/shard_map/ppermute | solution.py:15
  40.4 16.6 %collective-permute-start.4 = (bf16[128,16,128]{2,0,1:T(8,128)(2,1)S(1)}, bf16[128,16,128]{2,0,1:T(8,128)(2,1)S(1)}, u32[]{:S(2)}, u32[]{:S(2)}) collective-permute-start(bf16[128,16,128]{2,0,1:T(8,128)(2,1)S(1)} %copy.29), channel_id=1, source_target_pairs={{0,1},{1,2},{2,3},{3,4},{4,5},{5,6},{6,7},{7,8},{8,9},{9,10},{10,1... | collective-permute-start | bytes 1572872 | tf_op jit(solution)/shard_map/ppermute | solution.py:15
  57.0 3.5 %copy-start.6 = (bf16[128,16,128]{2,0,1:T(8,128)(2,1)}, bf16[128,16,128]{2,0,1:T(8,128)(2,1)S(1)}, u32[]{:S(2)}) copy-start(bf16[128,16,128]{2,0,1:T(8,128)(2,1)S(1)} %collective-permute-done.4) | copy-start | bytes 1572868
  60.5 2.9 %copy-start.2 = (f32[16,128,384]{2,1,0:T(8,128)}, f32[16,128,384]{2,1,0:T(8,128)S(1)}, u32[]{:S(2)}) copy-start(f32[16,128,384]{2,1,0:T(8,128)S(1)} %get-tuple-element.28) | copy-start | bytes 9437188
  64.4 2.8 %copy-start.3 = (f32[16,128,384]{2,1,0:T(8,128)S(1)}, f32[16,128,384]{2,1,0:T(8,128)}, u32[]{:S(2)}) copy-start(f32[16,128,384]{2,1,0:T(8,128)} %copy-done.2) | copy-start | bytes 9437188
  67.2 11.1 %copy-start.1 = (f32[384,16,128]{0,2,1:T(8,128)}, f32[384,16,128]{0,2,1:T(8,128)S(1)}, u32[]{:S(2)}) copy-start(f32[384,16,128]{0,2,1:T(8,128)S(1)} %convolution_bitcast_fusion) | copy-start | bytes 9437188
  71.1 8.9 %copy-start = (f32[384,16,128]{0,2,1:T(8,128)}, f32[384,16,128]{0,2,1:T(8,128)S(1)}, u32[]{:S(2)}) copy-start(f32[384,16,128]{0,2,1:T(8,128)S(1)} %multiply_bitcast_fusion) | copy-start | bytes 9437188
  73.0 14.2 %copy-start.7 = (bf16[128,16,128]{2,0,1:T(8,128)(2,1)S(1)}, bf16[128,16,128]{2,0,1:T(8,128)(2,1)}, u32[]{:S(2)}) copy-start(bf16[128,16,128]{2,0,1:T(8,128)(2,1)} %copy-done.6) | copy-start | bytes 1572868
  73.0 137.7 %collective-permute-start.6 = (f32[128,16,128]{0,2,1:T(8,128)}, f32[128,16,128]{0,2,1:T(8,128)}, u32[]{:S(2)}, u32[]{:S(2)}) collective-permute-start(f32[128,16,128]{0,2,1:T(8,128)} %get-tuple-element.21), channel_id=1, source_target_pairs={{0,63},{1,0},{2,1},{3,2},{4,3},{5,4},{6,5},{7,6},{8,7},{9,8},{10,9... | collective-permute-start | bytes 3145736 | tf_op jit(solution)/shard_map/ppermute | solution.py:15
  75.0 135.6 %collective-permute-start.7 = (f32[128,16,128]{0,2,1:T(8,128)}, f32[128,16,128]{0,2,1:T(8,128)}, u32[]{:S(2)}, u32[]{:S(2)}) collective-permute-start(f32[128,16,128]{0,2,1:T(8,128)} %get-tuple-element.22), channel_id=1, source_target_pairs={{0,1},{1,2},{2,3},{3,4},{4,5},{5,6},{6,7},{7,8},{8,9},{9,10},{10,1... | collective-permute-start | bytes 3145736 | tf_op jit(solution)/shard_map/ppermute | solution.py:15
  80.0 133.7 %collective-permute-start.8 = (f32[128,16,128]{0,2,1:T(8,128)}, f32[128,16,128]{0,2,1:T(8,128)S(1)}, u32[]{:S(2)}, u32[]{:S(2)}) collective-permute-start(f32[128,16,128]{0,2,1:T(8,128)} %get-tuple-element.19), channel_id=1, source_target_pairs={{0,63},{1,0},{2,1},{3,2},{4,3},{5,4},{6,5},{7,6},{8,7},{9,8},{10,9... | collective-permute-start | bytes 3145736 | tf_op jit(solution)/shard_map/ppermute | solution.py:15
  85.2 128.5 %collective-permute-start.9 = (f32[128,16,128]{0,2,1:T(8,128)}, f32[128,16,128]{0,2,1:T(8,128)}, u32[]{:S(2)}, u32[]{:S(2)}) collective-permute-start(f32[128,16,128]{0,2,1:T(8,128)} %get-tuple-element.20), channel_id=1, source_target_pairs={{0,1},{1,2},{2,3},{3,4},{4,5},{5,6},{6,7},{7,8},{8,9},{9,10},{10,1... | collective-permute-start | bytes 3145736 | tf_op jit(solution)/shard_map/ppermute | solution.py:15
where the time goes:
time: 217 us; the launch traced here: 216 us
  blocking collectives  120 us (55%)
  starting transfers between devices  46.1 us (21%)
  waiting for transfers between devices  14.6 us (7%)
  matrix products  13.2 us (6%)
  local copies, waits for them, and re-layouts  13 us (6%)
  other arithmetic  7.46 us (3%)
  between operations  2.29 us (1%)
    psum x1, blocking collectives, on_device(): gain_grad = lax.psum(gain_part, ('dp', 'view'))  120 us
    ppermute x10, starting transfers between devices, shifted(): lax.ppermute(array, axis, [(i, (i + by) % count) for i in range(count)])  46.1 us
    ppermute x10, waiting for transfers between devices, shifted(): lax.ppermute(array, axis, [(i, (i + by) % count) for i in range(count)])  14.6 us
    unnamed x26, local copies, waits for them, and re-layouts  6.85 us
  transfers between devices with their start and end apart: 10, of which 2 were waited for; matrix products, arithmetic and copies ran while one was open for 7% of the time, Pallas kernels for 0%

commit v1 on v0

v1 whole, which is shorter than its diff:
```python
import jax
import jax.numpy as jnp
from jax import lax
from jax.experimental import pallas as pl
from jax.experimental.pallas import tpu as pltpu
from jax.sharding import PartitionSpec as P

HEAD_DIM = 128
DEAD = -1e30
EPS = 1e-06
PER_STEP = 4
STATS = 4
MASK_ROWS = 16
RING = 8
NT = (((1,), (1,)), ((), ()))
NN = (((1,), (0,)), ((), ()))


def dot(a, b, dims):
    return lax.dot_general(a, b, dims, preferred_element_type=jnp.float32)


def shifted(array, axis, by):
    count = lax.axis_size(axis)
    return lax.ppermute(array, axis, [(i, (i + by) % count) for i in range(count)])


def columns_of(i):
    return slice(i * HEAD_DIM, (i + 1) * HEAD_DIM)


def head(ref, i):
    return ref[0, :, columns_of(i)]


def heads_of(refs, i):
    return jnp.concatenate([head(r, i) for r in refs], axis=0)


def pack_kernel(own_ref, k_ref, v_ref, out_ref):
    strip, width = k_ref.shape[1:]
    out_ref[0, :strip, :] = k_ref[0]
    out_ref[0, strip : 2 * strip, :] = v_ref[0]
    at = lax.broadcasted_iota(jnp.int32, (MASK_ROWS, width), 1)
    valid = (at >= own_ref[0]) & (at < own_ref[1])
    out_ref[0, 2 * strip :, :] = valid.astype(jnp.float32).astype(jnp.bfloat16)


def norm_kernel(q_ref, do_ref, gain_ref, out_ref):
    step = pl.program_id(0)
    strip = q_ref.shape[1]
    for i in range(PER_STEP):
        q = head(q_ref, i).astype(jnp.float32)
        gain = gain_ref[pl.ds(step * PER_STEP + i, 1), :]
        scale = lax.rsqrt(jnp.mean(q * q, axis=-1, keepdims=True) + EPS)
        out_ref[0, :strip, columns_of(i)] = (q * scale * gain).astype(jnp.bfloat16)
    out_ref[0, strip:, :] = do_ref[0]


def query_kernel(
    tasks_ref, own_ref,
    q_ref, n_ref, do_ref, k0_ref, v0_ref, k1_ref, v1_ref, m1_ref, k2_ref, v2_ref, m2_ref, gain_ref,
    att_ref, qgrad_ref, gpart_ref, stats_ref,
):
    step = pl.program_id(0)
    strip = q_ref.shape[1]
    inv = 1.0 / (HEAD_DIM**0.5)
    at = lax.broadcasted_iota(jnp.int32, (1, strip), 1)
    flags = (tasks_ref[0] > 0).astype(jnp.float32), (tasks_ref[1] > 0).astype(jnp.float32)
    own = ((at >= own_ref[0]) & (at < own_ref[1])).astype(jnp.float32)
    left = m1_ref[0, 0:1, :].astype(jnp.float32) * flags[0]
    right = m2_ref[0, 0:1, :].astype(jnp.float32) * flags[1]
    live = jnp.concatenate([own, left, right], axis=1) > 0.5
    lane = lax.broadcasted_iota(jnp.int32, (strip, 128), 1)
    columns = jnp.full((strip, 128), flags[0] + 2.0 * flags[1], jnp.float32)
    keys, values = (k0_ref, k1_ref, k2_ref), (v0_ref, v1_ref, v2_ref)
    each = range(PER_STEP)
    scores = [dot(head(n_ref, i), heads_of(keys, i), NT) for i in each]
    dprob = [dot(head(do_ref, i), heads_of(values, i), NT) for i in each]
    prob_b, dscore = [], []
    for i in each:
        masked = jnp.where(live, scores[i] * inv, DEAD)
        rowmax = jnp.max(masked, axis=-1, keepdims=True)
        expo = jnp.exp(masked - rowmax)
        share = 1.0 / jnp.sum(expo, axis=-1, keepdims=True)
        prob = expo * share
        delta = jnp.sum(prob * dprob[i], axis=-1, keepdims=True)
        prob_b.append(prob.astype(jnp.bfloat16))
        dscore.append((prob * (dprob[i] - delta)).astype(jnp.bfloat16))
        for j, stat in enumerate((rowmax, share, delta)):
            columns = jnp.where(lane == i * STATS + j, stat, columns)
    dnormed = [dot(dscore[i], heads_of(keys, i), NN) * inv for i in each]
    for i in each:
        att_ref[0, :, columns_of(i)] = dot(prob_b[i], heads_of(values, i), NN).astype(jnp.bfloat16)
    for i in each:
        row = pl.ds(step * PER_STEP + i, 1)
        gain = gain_ref[row, :]
        q = head(q_ref, i).astype(jnp.float32)
        scale = lax.rsqrt(jnp.mean(q * q, axis=-1, keepdims=True) + EPS)
        inner = jnp.sum(q * gain * dnormed[i], axis=-1, keepdims=True)
        cubed = scale * scale * scale
        qgrad = gain * scale * dnormed[i] - q * (cubed * inner * (1.0 / HEAD_DIM))
        qgrad_ref[0, :, columns_of(i)] = qgrad.astype(jnp.bfloat16)
        gpart_ref[row, :] = jnp.sum(q * scale * dnormed[i], axis=0, keepdims=True)
    stats_ref[...] = columns.T[: PER_STEP * STATS, :]


def key_kernel(
    own_ref,
    k_ref, v_ref, n0_ref, d0_ref, n1_ref, d1_ref, n2_ref, d2_ref, s0_ref, s1_ref, s2_ref,
    kgrad_ref, vgrad_ref,
):
    strip = k_ref.shape[1]
    inv = 1.0 / (HEAD_DIM**0.5)
    at = lax.broadcasted_iota(jnp.int32, (strip, 1), 0)
    valid = (at >= own_ref[0]) & (at < own_ref[1])
    left = s1_ref[3:4, :] >= 1.5
    right_flags = s2_ref[3:4, :]
    right = (right_flags == 1.0) | (right_flags == 3.0)
    live = jnp.concatenate(
        [jnp.broadcast_to(valid, (strip, strip)), valid & left, valid & right], axis=1
    )
    normed, dout = (n0_ref, n1_ref, n2_ref), (d0_ref, d1_ref, d2_ref)
    each = range(PER_STEP)
    scores = [dot(head(k_ref, i), heads_of(normed, i), NT) for i in each]
    dprob = [dot(head(v_ref, i), heads_of(dout, i), NT) for i in each]
    prob_b, dscore = [], []
    for i in each:
        rowmax, share, delta = (
            jnp.concatenate(
                [r[i * STATS + j : i * STATS + j + 1, :] for r in (s0_ref, s1_ref, s2_ref)], axis=1
            )
            for j in range(3)
        )
        masked = jnp.where(live, scores[i] * inv, DEAD)
        prob = jnp.exp(masked - rowmax) * share
        prob_b.append(prob.astype(jnp.bfloat16))
        dscore.append((prob * (dprob[i] - delta)).astype(jnp.bfloat16))
    for i in each:
        vgrad_ref[0, :, columns_of(i)] = dot(prob_b[i], heads_of(dout, i), NN).astype(jnp.bfloat16)
    for i in each:
        kgrad = dot(dscore[i], heads_of(normed, i), NN) * inv
        kgrad_ref[0, :, columns_of(i)] = kgrad.astype(jnp.bfloat16)


def total_over(part, axis, groups=None):
    count = lax.axis_size(axis) if groups is None else len(groups[0])
    if count == 1:
        return part
    blocks = jnp.broadcast_to(part[None], (count, *part.shape))
    blocks = lax.all_to_all(blocks, axis, 0, 0, axis_index_groups=groups, tiled=True)
    return jnp.sum(blocks, axis=0)


def on_device(queries, keys, values, out_grad, gain, tasks, bounds):
    _, strip, width = queries.shape
    heads = width // HEAD_DIM
    steps = heads // PER_STEP
    cols = PER_STEP * HEAD_DIM
    first = pl.BlockSpec((1, strip, cols), lambda i: (0, 0, i))
    second = pl.BlockSpec((1, strip, cols), lambda i: (0, 1, i))
    mask = pl.BlockSpec((1, MASK_ROWS, strip), lambda i: (0, 2 * strip // MASK_ROWS, 0))
    whole = pl.BlockSpec((heads, HEAD_DIM), lambda i: (0, 0))
    stat_block = pl.BlockSpec((PER_STEP * STATS, strip), lambda i: (i, 0))
    scalars = pl.BlockSpec(memory_space=pltpu.SMEM)
    wide = jax.ShapeDtypeStruct(queries.shape, jnp.bfloat16)
    params = pltpu.CompilerParams(vmem_limit_bytes=56 * 1024 * 1024)
    own_bounds, own_tasks = bounds.reshape(2), tasks.reshape(2)

    rows = 2 * strip + MASK_ROWS
    packed = pl.pallas_call(
        pack_kernel,
        grid=(steps,),
        in_specs=[scalars, first, first],
        out_specs=pl.BlockSpec((1, rows, cols), lambda i: (0, 0, i)),
        out_shape=jax.ShapeDtypeStruct((1, rows, width), jnp.bfloat16),
        compiler_params=params,
    )(own_bounds, keys, values)
    kv_left, kv_right = shifted(packed, "view", 1), shifted(packed, "view", -1)
    nd = pl.pallas_call(
        norm_kernel,
        grid=(steps,),
        in_specs=[first, first, whole],
        out_specs=pl.BlockSpec((1, 2 * strip, cols), lambda i: (0, 0, i)),
        out_shape=jax.ShapeDtypeStruct((1, 2 * strip, width), jnp.bfloat16),
        compiler_params=params,
    )(queries, out_grad, gain)
    nd_left, nd_right = shifted(nd, "view", 1), shifted(nd, "view", -1)

    mac = strip * strip * width
    attended, qgrad, gain_part, stats = pl.pallas_call(
        query_kernel,
        grid=(steps,),
        in_specs=[scalars] * 2 + [first] * 5 + [first, second, mask] * 2 + [whole],
        out_specs=[first, first, whole, stat_block],
        out_shape=[
            wide,
            wide,
            jax.ShapeDtypeStruct((heads, HEAD_DIM), jnp.float32),
            jax.ShapeDtypeStruct((heads * STATS, strip), jnp.float32),
        ],
        compiler_params=params,
        cost_estimate=pl.CostEstimate(
            flops=24 * mac, bytes_accessed=22 * strip * width, transcendentals=3 * heads * strip * strip
        ),
    )(
        own_tasks, own_bounds, queries, nd, out_grad, keys, values,
        kv_left, kv_left, kv_left, kv_right, kv_right, kv_right, gain,
    )
    s_left, s_right = shifted(stats, "view", 1), shifted(stats, "view", -1)

    count = lax.axis_size("view")
    ring = RING if count % RING == 0 else count
    across = [[y * ring + z for y in range(count // ring)] for z in range(ring)]
    along = [[y * ring + z for z in range(ring)] for y in range(count // ring)]
    gain_grad = total_over(gain_part, "dp")
    gain_grad = total_over(gain_grad, "view", across)
    gain_grad = total_over(gain_grad, "view", along)

    kgrad, vgrad = pl.pallas_call(
        key_kernel,
        grid=(steps,),
        in_specs=[scalars] + [first] * 2 + [first, second] * 3 + [stat_block] * 3,
        out_specs=[first, first],
        out_shape=[wide, wide],
        compiler_params=params,
        cost_estimate=pl.CostEstimate(
            flops=24 * mac, bytes_accessed=20 * strip * width, transcendentals=3 * heads * strip * strip
        ),
    )(
        own_bounds, keys, values, nd, nd, nd_left, nd_left, nd_right, nd_right, stats, s_left, s_right
    )
    return attended, qgrad, kgrad, vgrad, gain_grad


def solution(mesh):
    rows = P("dp", "view", None)
    return jax.shard_map(
        on_device,
        mesh=mesh,
        in_specs=(rows, rows, rows, rows, P(), rows, rows),
        out_specs=(rows, rows, rows, rows, P()),
        check_vma=False,
    )
```

time: 217 us -> 99.7 us (0.46)
  blocking collectives: 120 us -> 22.9 us
  Pallas kernels: 0 us -> 19.4 us
  matrix products: 13.2 us -> 0 us
  local copies, waits for them, and re-layouts: 13 us -> 3.01 us
  starting transfers between devices: 46.1 us -> 39 us
  other arithmetic: 7.46 us -> 0.63 us
  waiting for transfers between devices: 14.6 us -> 12.4 us
    psum x1 -> x0, blocking collectives: 120 us -> none  [on_device(): gain_grad = lax.psum(gain_part, ('dp', 'view'))]
    all_to_all x0 -> x2, blocking collectives: none -> 22.9 us  [total_over(): lax.all_to_all(blocks, axis, 0, 0, axis_index_groups=groups, tiled=True)]
    pallas_call x0 -> x4, Pallas kernels: none -> 19.4 us  [the longest x1 6.35 us: on_device(): pl.pallas_call(query_kernel, grid=(steps,), in_specs=[scalars] * 2 + [fir...]
    dot_general x6 -> x0, matrix products: 13.2 us -> none  [the longest x1 2.89 us: on_device(): jnp.einsum('hqk,khd->qhd', prob_b, values_all, preferred_element_type=jnp...]
    ppermute x10 -> x6, starting transfers between devices: 46.1 us -> 33.5 us  [shifted(): lax.ppermute(array, axis, [(i, (i + by) % count) for i in range(count)])]
    convert_element_type x5 -> x0, other arithmetic: 6.15 us -> none  [the longest x1 2.04 us: on_device(): ktotal.astype(jnp.bfloat16).reshape(flat)]
    all_to_all x0 -> x1, starting transfers between devices: none -> 5.47 us  [total_over(): lax.all_to_all(blocks, axis, 0, 0, axis_index_groups=groups, tiled=True)]
    slice x4 -> x0, local copies, waits for them, and re-layouts: 5.36 us -> none  [the longest x1 1.85 us: on_device(): kgrad[low:low + strip]]
  transfers between devices with their start and end apart: 10 -> 7, of which waited for: 2 -> 3; matrix products, arithmetic and copies ran while one was open for 7% -> 1% of each run, Pallas kernels for 0% -> 16%
where the time goes in v1:
time: 99.7 us; the launch traced here: 98.1 us
  starting transfers between devices  39 us (39%)
  blocking collectives  22.9 us (23%)
  Pallas kernels  19.4 us (19%)
  waiting for transfers between devices  12.4 us (12%)
  local copies, waits for them, and re-layouts  3.01 us (3%)
    ppermute x6, starting transfers between devices, shifted(): lax.ppermute(array, axis, [(i, (i + by) % count) for i in range(count)])  33.5 us
    all_to_all x2, blocking collectives, total_over(): lax.all_to_all(blocks, axis, 0, 0, axis_index_groups=groups, tiled=True)  22.9 us
    ppermute x6, waiting for transfers between devices, shifted(): lax.ppermute(array, axis, [(i, (i + by) % count) for i in range(count)])  12.4 us
    pallas_call x1, Pallas kernels, on_device(): pl.pallas_call(query_kernel, grid=(steps,), in_specs=[scalars] * 2 + [fir...  6.35 us
    pallas_call x1, Pallas kernels, on_device(): pl.pallas_call(key_kernel, grid=(steps,), in_specs=[scalars] + [first] *...  5.8 us
    all_to_all x1, starting transfers between devices, total_over(): lax.all_to_all(blocks, axis, 0, 0, axis_index_groups=groups, tiled=True)  5.47 us
    pallas_call x1, Pallas kernels, on_device(): pl.pallas_call(norm_kernel, grid=(steps,), in_specs=[first, first, whole]...  3.77 us
    pallas_call x1, Pallas kernels, on_device(): pl.pallas_call(pack_kernel, grid=(steps,), in_specs=[scalars, first, firs...  3.5 us
  transfers between devices with their start and end apart: 7, of which 3 were waited for; matrix products, arithmetic and copies ran while one was open for 1% of the time, Pallas kernels for 16%

profile of v1, /device:TPU:1, one launch (start us, length us, event | category | flops | bytes accessed | tf_op | source)
XLA Modules:
  0.0 98.1 jit_solution(10648369733634875003)
XLA Ops:
  0.6 3.5 %shard_map.111 = bf16[1,272,2048]{2,1,0:T(8,128)(2,1)} custom-call(s32[2]{0:T(128)} %bitcast.2, bf16[1,128,2048]{2,1,0:T(8,128)(2,1)} %k_ref.3, bf16[1,128,2048]{2,1,0:T(8,128)(2,1)} %v_ref.3), custom_call_target="tpu_custom_call" | custom-call | tf_op jit(solution)/shard_map/pallas_call | solution.py:171
  4.1 4.8 %collective-permute-start = (bf16[1,272,2048]{2,1,0:T(8,128)(2,1)}, bf16[1,272,2048]{2,1,0:T(8,128)(2,1)S(1)}, u32[]{:S(2)}, u32[]{:S(2)}) collective-permute-start(bf16[1,272,2048]{2,1,0:T(8,128)(2,1)} %shard_map.111), channel_id=1, source_target_pairs={{0,1},{1,2},{2,3},{3,4},{4,5},{5,6},{6,7},{7,8},{8,9},{9,10},{10,1... | collective-permute-start | bytes 3342344 | tf_op jit(solution)/shard_map/ppermute | solution.py:25
  9.0 11.5 %collective-permute-start.1 = (bf16[1,272,2048]{2,1,0:T(8,128)(2,1)}, bf16[1,272,2048]{2,1,0:T(8,128)(2,1)S(1)}, u32[]{:S(2)}, u32[]{:S(2)}) collective-permute-start(bf16[1,272,2048]{2,1,0:T(8,128)(2,1)} %shard_map.111), channel_id=1, source_target_pairs={{0,63},{1,0},{2,1},{3,2},{4,3},{5,4},{6,5},{7,6},{8,7},{9,8},{10,9... | collective-permute-start | bytes 3342344 | tf_op jit(solution)/shard_map/ppermute | solution.py:25
  20.5 3.8 %shard_map.110.n_ref.n0_ref.d0_ref = bf16[1,256,2048]{2,1,0:T(8,128)(2,1)} custom-call(bf16[1,128,2048]{2,1,0:T(8,128)(2,1)} %q_ref.3, bf16[1,128,2048]{2,1,0:T(8,128)(2,1)} %do_ref.3, f32[16,128]{1,0:T(8,128)} %gain_ref.3), custom_call_target="tpu_custom_call" | custom-call | tf_op jit(solution)/shard_map/pallas_call | solution.py:180
  24.2 1.9 %collective-permute-start.2 = (bf16[1,256,2048]{2,1,0:T(8,128)(2,1)}, bf16[1,256,2048]{2,1,0:T(8,128)(2,1)S(1)}, u32[]{:S(2)}, u32[]{:S(2)}) collective-permute-start(bf16[1,256,2048]{2,1,0:T(8,128)(2,1)} %shard_map.110.n_ref.n0_ref.d0_ref), channel_id=1, source_target_pairs={{0,1},{1,2},{2,3},{3,4},{4,5},{5,6},{6,7},{7,8},{8,9},{9,10},{10,1... | collective-permute-start | bytes 3145736 | tf_op jit(solution)/shard_map/ppermute | solution.py:25
  26.1 6.7 %collective-permute-start.3 = (bf16[1,256,2048]{2,1,0:T(8,128)(2,1)}, bf16[1,256,2048]{2,1,0:T(8,128)(2,1)S(1)}, u32[]{:S(2)}, u32[]{:S(2)}) collective-permute-start(bf16[1,256,2048]{2,1,0:T(8,128)(2,1)} %shard_map.110.n_ref.n0_ref.d0_ref), channel_id=1, source_target_pairs={{0,63},{1,0},{2,1},{3,2},{4,3},{5,4},{6,5},{7,6},{8,7},{9,8},{10,9... | collective-permute-start | bytes 3145736 | tf_op jit(solution)/shard_map/ppermute | solution.py:25
  32.8 10.2 %collective-permute-done.k1_ref.v1_ref.m1_ref = bf16[1,272,2048]{2,1,0:T(8,128)(2,1)S(1)} collective-permute-done((bf16[1,272,2048]{2,1,0:T(8,128)(2,1)}, bf16[1,272,2048]{2,1,0:T(8,128)(2,1)S(1)}, u32[]{:S(2)}, u32[]{:S(2)}) %collective-permute-start) | collective-permute-done | bytes 1114144 | tf_op jit(solution)/shard_map/ppermute | solution.py:25
  43.0 1.0 collective-permute-done.1.k2_ref.v2_ref.m2_ref
  44.0 0.0 copy-done
  44.0 1.0 %copy-done.1 = bf16[1,272,2048]{2,1,0:T(8,128)(2,1)} copy-done((bf16[1,272,2048]{2,1,0:T(8,128)(2,1)}, bf16[1,272,2048]{2,1,0:T(8,128)(2,1)S(1)}, u32[]{:S(2)}) %copy-start.1) | copy-done | bytes 1114136
  45.0 6.4 %shard_map.112 = (bf16[1,128,2048]{2,1,0:T(8,128)(2,1)}, bf16[1,128,2048]{2,1,0:T(8,128)(2,1)}, f32[16,128]{1,0:T(8,128)}, f32[64,128]{1,0:T(8,128)}) custom-call(s32[2]{0:T(128)} %bitcast.5, s32[2]{0:T(128)} %bitcast.3, bf16[1,128,2048]{2,1,0:T(8,128)(2,1)} %q_ref.3, bf16[1,256,2048]{2,1,0:T(8,128)(2,1)} %shard_map.110.n_ref.n0_ref.d0_ref, ...), custom_call_target="tpu_custom_call" | custom-call | flops 805306368 | bytes 5767168 | tf_op jit(solution)/shard_map/pallas_call | solution.py:191
  51.4 0.7 broadcast_in_dim.6
  52.1 11.9 %all_to_all.15 = f32[8,16,128]{2,1,0:T(8,128)S(1)} all-to-all(f32[8,16,128]{2,1,0:T(8,128)S(1)} %broadcast_in_dim.6), channel_id=1, replica_groups=mesh['dp'=8,'view'=64] {'dp'}, dimensions={0} | all-to-all | bytes 131072 | tf_op jit(solution)/shard_map/all_to_all | solution.py:151
  64.0 11.0 %all_to_all.16 = f32[8,16,128]{2,1,0:T(8,128)S(1)} all-to-all(f32[8,16,128]{2,1,0:T(8,128)S(1)} %broadcast_in_dim.7), channel_id=1, replica_groups={{0,8,16,24,32,40,48,56},{1,9,17,25,33,41,49,57},{2,10,18,26,34,42,50,58..., dimensions={0} | all-to-all | bytes 131072 | tf_op jit(solution)/shard_map/all_to_all | solution.py:151
  75.0 0.6 broadcast_in_dim.8
  75.6 5.5 %all-to-all-start.2 = ((f32[8,16,128]{2,1,0:T(8,128)}), f32[8,16,128]{2,1,0:T(8,128)S(1)}, u32[]{:S(2)}, u32[]{:S(2)}) async-start(f32[8,16,128]{2,1,0:T(8,128)} %broadcast_in_dim.8), calls=%async_computation.2 | async-start | bytes 131072 | tf_op jit(solution)/shard_map/all_to_all | solution.py:151
  81.1 3.4 %collective-permute-start.4 = (f32[64,128]{1,0:T(8,128)}, f32[64,128]{1,0:T(8,128)S(1)}, u32[]{:S(2)}, u32[]{:S(2)}) collective-permute-start(f32[64,128]{1,0:T(8,128)} %get-tuple-element.13.s0_ref), channel_id=1, source_target_pairs={{0,1},{1,2},{2,3},{3,4},{4,5},{5,6},{6,7},{7,8},{8,9},{9,10},{10,1... | collective-permute-start | bytes 98312 | tf_op jit(solution)/shard_map/ppermute | solution.py:25
  84.4 5.2 %collective-permute-start.5 = (f32[64,128]{1,0:T(8,128)}, f32[64,128]{1,0:T(8,128)S(1)}, u32[]{:S(2)}, u32[]{:S(2)}) collective-permute-start(f32[64,128]{1,0:T(8,128)} %get-tuple-element.13.s0_ref), channel_id=1, source_target_pairs={{0,63},{1,0},{2,1},{3,2},{4,3},{5,4},{6,5},{7,6},{8,7},{9,8},{10,9... | collective-permute-start | bytes 98312 | tf_op jit(solution)/shard_map/ppermute | solution.py:25
  89.7 0.0 collective-permute-done.3.n2_ref.d2_ref
  89.7 1.3 %collective-permute-done.5.s2_ref = f32[64,128]{1,0:T(8,128)S(1)} collective-permute-done((f32[64,128]{1,0:T(8,128)}, f32[64,128]{1,0:T(8,128)S(1)}, u32[]{:S(2)}, u32[]{:S(2)}) %collective-permute-start.5) | collective-permute-done | bytes 32800 | tf_op jit(solution)/shard_map/ppermute | solution.py:25
  91.0 0.0 copy-done.3
  91.0 0.6 copy-done.5
  91.7 5.8 %shard_map.113 = (bf16[1,128,2048]{2,1,0:T(8,128)(2,1)}, bf16[1,128,2048]{2,1,0:T(8,128)(2,1)}) custom-call(s32[2]{0:T(128)} %bitcast.4, bf16[1,128,2048]{2,1,0:T(8,128)(2,1)} %k_ref.3, bf16[1,128,2048]{2,1,0:T(8,128)(2,1)} %v_ref.3, bf16[1,256,2048]{2,1,0:T(8,128)(2,1)} %shard_map.110.n_ref.n0_ref.d0_ref, ...), custom_call_target="tpu_custom_call" | custom-call | flops 805306368 | bytes 5242880 | tf_op jit(solution)/shard_map/pallas_call | solution.py:220
  97.5 0.6 reduce_sum.29
  (14 shorter events, 0.1 us)
Async XLA Ops:
  4.1 38.9 %collective-permute-start = (bf16[1,272,2048]{2,1,0:T(8,128)(2,1)}, bf16[1,272,2048]{2,1,0:T(8,128)(2,1)S(1)}, u32[]{:S(2)}, u32[]{:S(2)}) collective-permute-start(bf16[1,272,2048]{2,1,0:T(8,128)(2,1)} %shard_map.111), channel_id=1, source_target_pairs={{0,1},{1,2},{2,3},{3,4},{4,5},{5,6},{6,7},{7,8},{8,9},{9,10},{10,1... | collective-permute-start | bytes 3342344 | tf_op jit(solution)/shard_map/ppermute | solution.py:25
  9.0 35.0 %collective-permute-start.1 = (bf16[1,272,2048]{2,1,0:T(8,128)(2,1)}, bf16[1,272,2048]{2,1,0:T(8,128)(2,1)S(1)}, u32[]{:S(2)}, u32[]{:S(2)}) collective-permute-start(bf16[1,272,2048]{2,1,0:T(8,128)(2,1)} %shard_map.111), channel_id=1, source_target_pairs={{0,63},{1,0},{2,1},{3,2},{4,3},{5,4},{6,5},{7,6},{8,7},{9,8},{10,9... | collective-permute-start | bytes 3342344 | tf_op jit(solution)/shard_map/ppermute | solution.py:25
  24.2 65.4 %collective-permute-start.2 = (bf16[1,256,2048]{2,1,0:T(8,128)(2,1)}, bf16[1,256,2048]{2,1,0:T(8,128)(2,1)S(1)}, u32[]{:S(2)}, u32[]{:S(2)}) collective-permute-start(bf16[1,256,2048]{2,1,0:T(8,128)(2,1)} %shard_map.110.n_ref.n0_ref.d0_ref), channel_id=1, source_target_pairs={{0,1},{1,2},{2,3},{3,4},{4,5},{5,6},{6,7},{7,8},{8,9},{9,10},{10,1... | collective-permute-start | bytes 3145736 | tf_op jit(solution)/shard_map/ppermute | solution.py:25
  26.1 63.6 %collective-permute-start.3 = (bf16[1,256,2048]{2,1,0:T(8,128)(2,1)}, bf16[1,256,2048]{2,1,0:T(8,128)(2,1)S(1)}, u32[]{:S(2)}, u32[]{:S(2)}) collective-permute-start(bf16[1,256,2048]{2,1,0:T(8,128)(2,1)} %shard_map.110.n_ref.n0_ref.d0_ref), channel_id=1, source_target_pairs={{0,63},{1,0},{2,1},{3,2},{4,3},{5,4},{6,5},{7,6},{8,7},{9,8},{10,9... | collective-permute-start | bytes 3145736 | tf_op jit(solution)/shard_map/ppermute | solution.py:25
  43.0 1.0 %copy-start = (bf16[1,272,2048]{2,1,0:T(8,128)(2,1)}, bf16[1,272,2048]{2,1,0:T(8,128)(2,1)S(1)}, u32[]{:S(2)}) copy-start(bf16[1,272,2048]{2,1,0:T(8,128)(2,1)S(1)} %collective-permute-done.k1_ref.v1_ref.m1_ref) | copy-start | bytes 3342340
  44.0 1.0 %copy-start.1 = (bf16[1,272,2048]{2,1,0:T(8,128)(2,1)}, bf16[1,272,2048]{2,1,0:T(8,128)(2,1)S(1)}, u32[]{:S(2)}) copy-start(bf16[1,272,2048]{2,1,0:T(8,128)(2,1)S(1)} %collective-permute-done.1.k2_ref.v2_ref.m2_ref) | copy-start | bytes 3342340
  75.6 21.9 %all-to-all-start.2 = ((f32[8,16,128]{2,1,0:T(8,128)}), f32[8,16,128]{2,1,0:T(8,128)S(1)}, u32[]{:S(2)}, u32[]{:S(2)}) async-start(f32[8,16,128]{2,1,0:T(8,128)} %broadcast_in_dim.8), calls=%async_computation.2 | async-start | bytes 131072 | tf_op jit(solution)/shard_map/all_to_all | solution.py:151
  81.1 8.6 %collective-permute-start.4 = (f32[64,128]{1,0:T(8,128)}, f32[64,128]{1,0:T(8,128)S(1)}, u32[]{:S(2)}, u32[]{:S(2)}) collective-permute-start(f32[64,128]{1,0:T(8,128)} %get-tuple-element.13.s0_ref), channel_id=1, source_target_pairs={{0,1},{1,2},{2,3},{3,4},{4,5},{5,6},{6,7},{7,8},{8,9},{9,10},{10,1... | collective-permute-start | bytes 98312 | tf_op jit(solution)/shard_map/ppermute | solution.py:25
  84.4 6.6 %collective-permute-start.5 = (f32[64,128]{1,0:T(8,128)}, f32[64,128]{1,0:T(8,128)S(1)}, u32[]{:S(2)}, u32[]{:S(2)}) collective-permute-start(f32[64,128]{1,0:T(8,128)} %get-tuple-element.13.s0_ref), channel_id=1, source_target_pairs={{0,63},{1,0},{2,1},{3,2},{4,3},{5,4},{6,5},{7,6},{8,7},{9,8},{10,9... | collective-permute-start | bytes 98312 | tf_op jit(solution)/shard_map/ppermute | solution.py:25
  89.7 1.3 %copy-start.2 = (bf16[1,256,2048]{2,1,0:T(8,128)(2,1)}, bf16[1,256,2048]{2,1,0:T(8,128)(2,1)S(1)}, u32[]{:S(2)}) copy-start(bf16[1,256,2048]{2,1,0:T(8,128)(2,1)S(1)} %collective-permute-done.2.n1_ref.d1_ref) | copy-start | bytes 3145732
  89.7 1.3 %copy-start.3 = (bf16[1,256,2048]{2,1,0:T(8,128)(2,1)}, bf16[1,256,2048]{2,1,0:T(8,128)(2,1)S(1)}, u32[]{:S(2)}) copy-start(bf16[1,256,2048]{2,1,0:T(8,128)(2,1)S(1)} %collective-permute-done.3.n2_ref.d2_ref) | copy-start | bytes 3145732
  89.7 1.3 %copy-start.4 = (f32[64,128]{1,0:T(8,128)}, f32[64,128]{1,0:T(8,128)S(1)}, u32[]{:S(2)}) copy-start(f32[64,128]{1,0:T(8,128)S(1)} %collective-permute-done.4.s1_ref) | copy-start | bytes 98308
  91.0 0.6 copy-start.5

commit v2 on v1

--- a/solution.py
+++ b/solution.py
@@ -1,3 +1,5 @@
+import functools
+
 import jax
 import jax.numpy as jnp
 from jax import lax
@@ -46,22 +48,29 @@
     out_ref[0, 2 * strip :, :] = valid.astype(jnp.float32).astype(jnp.bfloat16)
 
 
-def norm_kernel(q_ref, do_ref, gain_ref, out_ref):
+def prep_kernel(k_ref, v_ref, q_ref, do_ref, gain_ref, kv_ref, nd_ref):
     step = pl.program_id(0)
-    strip = q_ref.shape[1]
+    strip = k_ref.shape[1]
+    kv_ref[0, :strip, :] = k_ref[0]
+    kv_ref[0, strip:, :] = v_ref[0]
     for i in range(PER_STEP):
         q = head(q_ref, i).astype(jnp.float32)
         gain = gain_ref[pl.ds(step * PER_STEP + i, 1), :]
         scale = lax.rsqrt(jnp.mean(q * q, axis=-1, keepdims=True) + EPS)
-        out_ref[0, :strip, columns_of(i)] = (q * scale * gain).astype(jnp.bfloat16)
-    out_ref[0, strip:, :] = do_ref[0]
+        nd_ref[0, :strip, columns_of(i)] = (q * scale * gain).astype(jnp.bfloat16)
+    nd_ref[0, strip:, :] = do_ref[0]
 
 
 def query_kernel(
-    tasks_ref, own_ref,
+    start, tasks_ref, own_ref,
     q_ref, n_ref, do_ref, k0_ref, v0_ref, k1_ref, v1_ref, m1_ref, k2_ref, v2_ref, m2_ref, gain_ref,
-    att_ref, qgrad_ref, gpart_ref, stats_ref,
+    *rest,
 ):
+    att_ref, qgrad_ref, stats_ref, gpart_ref = rest[-4:]
+    if start:
+        gpart_ref[:, :start, :] = jnp.broadcast_to(
+            rest[3][...], (gpart_ref.shape[0], start, HEAD_DIM)
+        )
     step = pl.program_id(0)
     strip = q_ref.shape[1]
     inv = 1.0 / (HEAD_DIM**0.5)
@@ -93,7 +102,7 @@
     for i in each:
         att_ref[0, :, columns_of(i)] = dot(prob_b[i], heads_of(values, i), NN).astype(jnp.bfloat16)
     for i in each:
-        row = pl.ds(step * PER_STEP + i, 1)
+        row = pl.ds(start + step * PER_STEP + i, 1)
         gain = gain_ref[row, :]
         q = head(q_ref, i).astype(jnp.float32)
         scale = lax.rsqrt(jnp.mean(q * q, axis=-1, keepdims=True) + EPS)
@@ -101,7 +110,9 @@
         cubed = scale * scale * scale
         qgrad = gain * scale * dnormed[i] - q * (cubed * inner * (1.0 / HEAD_DIM))
         qgrad_ref[0, :, columns_of(i)] = qgrad.astype(jnp.bfloat16)
-        gpart_ref[row, :] = jnp.sum(q * scale * dnormed[i], axis=0, keepdims=True)
+        part = jnp.sum(q * scale * dnormed[i], axis=0, keepdims=True)
+        for j in range(gpart_ref.shape[0]):
+            gpart_ref[j, row, :] = part
     stats_ref[...] = columns.T[: PER_STEP * STATS, :]
 
 
@@ -143,13 +154,18 @@
         kgrad_ref[0, :, columns_of(i)] = kgrad.astype(jnp.bfloat16)
 
 
-def total_over(part, axis, groups=None):
-    count = lax.axis_size(axis) if groups is None else len(groups[0])
-    if count == 1:
-        return part
-    blocks = jnp.broadcast_to(part[None], (count, *part.shape))
-    blocks = lax.all_to_all(blocks, axis, 0, 0, axis_index_groups=groups, tiled=True)
+def total_over(blocks, axis, groups=None):
+    if blocks.shape[0] > 1:
+        blocks = lax.all_to_all(blocks, axis, 0, 0, axis_index_groups=groups, tiled=True)
     return jnp.sum(blocks, axis=0)
+
+
+def copies(part, count):
+    return jnp.broadcast_to(part[None], (count, *part.shape))
+
+
+def tied(value, *others):
+    return lax.optimization_barrier((value, *others))[0]
 
 
 def on_device(queries, keys, values, out_grad, gain, tasks, bounds):
@@ -157,79 +173,117 @@
     heads = width // HEAD_DIM
     steps = heads // PER_STEP
     cols = PER_STEP * HEAD_DIM
-    first = pl.BlockSpec((1, strip, cols), lambda i: (0, 0, i))
-    second = pl.BlockSpec((1, strip, cols), lambda i: (0, 1, i))
-    mask = pl.BlockSpec((1, MASK_ROWS, strip), lambda i: (0, 2 * strip // MASK_ROWS, 0))
-    whole = pl.BlockSpec((heads, HEAD_DIM), lambda i: (0, 0))
-    stat_block = pl.BlockSpec((PER_STEP * STATS, strip), lambda i: (i, 0))
-    scalars = pl.BlockSpec(memory_space=pltpu.SMEM)
-    wide = jax.ShapeDtypeStruct(queries.shape, jnp.bfloat16)
-    params = pltpu.CompilerParams(vmem_limit_bytes=56 * 1024 * 1024)
-    own_bounds, own_tasks = bounds.reshape(2), tasks.reshape(2)
-
-    rows = 2 * strip + MASK_ROWS
-    packed = pl.pallas_call(
-        pack_kernel,
-        grid=(steps,),
-        in_specs=[scalars, first, first],
-        out_specs=pl.BlockSpec((1, rows, cols), lambda i: (0, 0, i)),
-        out_shape=jax.ShapeDtypeStruct((1, rows, width), jnp.bfloat16),
-        compiler_params=params,
-    )(own_bounds, keys, values)
-    kv_left, kv_right = shifted(packed, "view", 1), shifted(packed, "view", -1)
-    nd = pl.pallas_call(
-        norm_kernel,
-        grid=(steps,),
-        in_specs=[first, first, whole],
-        out_specs=pl.BlockSpec((1, 2 * strip, cols), lambda i: (0, 0, i)),
-        out_shape=jax.ShapeDtypeStruct((1, 2 * strip, width), jnp.bfloat16),
-        compiler_params=params,
-    )(queries, out_grad, gain)
-    nd_left, nd_right = shifted(nd, "view", 1), shifted(nd, "view", -1)
-
-    mac = strip * strip * width
-    attended, qgrad, gain_part, stats = pl.pallas_call(
-        query_kernel,
-        grid=(steps,),
-        in_specs=[scalars] * 2 + [first] * 5 + [first, second, mask] * 2 + [whole],
-        out_specs=[first, first, whole, stat_block],
-        out_shape=[
-            wide,
-            wide,
-            jax.ShapeDtypeStruct((heads, HEAD_DIM), jnp.float32),
-            jax.ShapeDtypeStruct((heads * STATS, strip), jnp.float32),
-        ],
-        compiler_params=params,
-        cost_estimate=pl.CostEstimate(
-            flops=24 * mac, bytes_accessed=22 * strip * width, transcendentals=3 * heads * strip * strip
-        ),
-    )(
-        own_tasks, own_bounds, queries, nd, out_grad, keys, values,
-        kv_left, kv_left, kv_left, kv_right, kv_right, kv_right, gain,
-    )
-    s_left, s_right = shifted(stats, "view", 1), shifted(stats, "view", -1)
-
+    halves = 2
+    per_half = steps // halves
+    n_dp = lax.axis_size("dp")
     count = lax.axis_size("view")
     ring = RING if count % RING == 0 else count
+
+    def block(row, at=0, of=cols):
+        return pl.BlockSpec((1, strip, of), lambda i: (0, row, at + i))
+
+    whole = pl.BlockSpec((heads, HEAD_DIM), lambda i: (0, 0))
+    scalars = pl.BlockSpec(memory_space=pltpu.SMEM)
+    anywhere = pl.BlockSpec(memory_space=pl.ANY)
+    wide = jax.ShapeDtypeStruct(queries.shape, jnp.bfloat16)
+    own_bounds, own_tasks = bounds.reshape(2), tasks.reshape(2)
+    mac = strip * strip * width
+
+    def call(kernel, grid, in_specs, out_specs, out_shape, cost=0, aliases=None):
+        return pl.pallas_call(
+            kernel,
+            grid=(grid,),
+            in_specs=in_specs,
+            out_specs=out_specs,
+            out_shape=out_shape,
+            input_output_aliases=aliases or {},
+            name=(kernel.func if isinstance(kernel, functools.partial) else kernel).__name__,
+            compiler_params=pltpu.CompilerParams(vmem_limit_bytes=63 * 1024 * 1024),
+            cost_estimate=pl.CostEstimate(flops=cost * mac, bytes_accessed=8 * strip * width, transcendentals=0),
+        )
+
+    rows = 2 * strip + MASK_ROWS
+    kv0 = call(
+        pack_kernel,
+        per_half,
+        [scalars, block(0), block(0)],
+        pl.BlockSpec((1, rows, cols), lambda i: (0, 0, i)),
+        jax.ShapeDtypeStruct((1, rows, width // halves), jnp.bfloat16),
+    )(own_bounds, keys, values)
+    kv0_left, kv0_right = shifted(kv0, "view", 1), shifted(kv0, "view", -1)
+
+    thin = cols // halves
+    kv1, nd = call(
+        prep_kernel,
+        steps,
+        [block(0, steps, thin), block(0, steps, thin), block(0), block(0), whole],
+        [
+            pl.BlockSpec((1, 2 * strip, thin), lambda i: (0, 0, i)),
+            pl.BlockSpec((1, 2 * strip, cols), lambda i: (0, 0, i)),
+        ],
+        [
+            jax.ShapeDtypeStruct((1, 2 * strip, width // halves), jnp.bfloat16),
+            jax.ShapeDtypeStruct((1, 2 * strip, width), jnp.bfloat16),
+        ],
+        cost=140,
+    )(keys, values, queries, out_grad, gain)
+    kv1_left, kv1_right = shifted(kv1, "view", 1), shifted(kv1, "view", -1)
+
+    def query_side(half, left, right, before):
+        at = half * per_half
+        mask = pl.BlockSpec((1, MASK_ROWS, strip), lambda i: (0, 2 * strip // MASK_ROWS, 0))
+        near = [block(0), block(1), mask]
+        count, per = (1, heads // halves) if half == 0 else (n_dp, heads)
+        return call(
+            functools.partial(query_kernel, at * PER_STEP),
+            per_half,
+            [scalars] * 2 + [block(0, at)] * 5 + near * 2 + [whole]
+            + [anywhere] * (3 if half else 0)
+            + [pl.BlockSpec((1, heads // halves, HEAD_DIM), lambda i: (0, 0, 0))] * (1 if half else 0),
+            [
+                block(0, at),
+                block(0, at),
+                pl.BlockSpec((PER_STEP * STATS, strip), lambda i: (at + i, 0)),
+                pl.BlockSpec((count, per, HEAD_DIM), lambda i: (0, 0, 0)),
+            ],
+            [
+                wide,
+                wide,
+                jax.ShapeDtypeStruct((heads * STATS, strip), jnp.float32),
+                jax.ShapeDtypeStruct((count, per, HEAD_DIM), jnp.float32),
+            ],
+            cost=3000,
+            aliases={14: 0, 15: 1, 16: 2} if half else None,
+        )(
+            own_tasks, own_bounds, queries, nd, out_grad, keys, values,
+            left, left, kv0_left, right, right, kv0_right, gain, *before,
+        )
+
+    early = query_side(0, kv0_left, kv0_right, ())
+    attended, qgrad, stats, gain_parts = query_side(1, kv1_left, kv1_right, early)
+    nd_sent = nd
+    nd_left, nd_right = shifted(nd_sent, "view", 1), shifted(nd_sent, "view", -1)
+    s_left, s_right = shifted(stats, "view", 1), shifted(stats, "view", -1)
+
     across = [[y * ring + z for y in range(count // ring)] for z in range(ring)]
     along = [[y * ring + z for z in range(ring)] for y in range(count // ring)]
-    gain_grad = total_over(gain_part, "dp")
-    gain_grad = total_over(gain_grad, "view", across)
-    gain_grad = total_over(gain_grad, "view", along)
-
-    kgrad, vgrad = pl.pallas_call(
+    gain_grad = total_over(gain_parts, "dp")
+    gain_grad = total_over(copies(gain_grad, count // ring), "view", across)
+
+    own = [block(0), block(1)]
+    stat_block = pl.BlockSpec((PER_STEP * STATS, strip), lambda i: (i, 0))
+    kgrad, vgrad = call(
         key_kernel,
-        grid=(steps,),
-        in_specs=[scalars] + [first] * 2 + [first, second] * 3 + [stat_block] * 3,
-        out_specs=[first, first],
-        out_shape=[wide, wide],
-        compiler_params=params,
-        cost_estimate=pl.CostEstimate(
-            flops=24 * mac, bytes_accessed=20 * strip * width, transcendentals=3 * heads * strip * strip
-        ),
+        steps,
+        [scalars] + [block(0)] * 2 + own * 3 + [stat_block] * 3,
+        [block(0)] * 2,
+        [wide, wide],
+        cost=30,
     )(
         own_bounds, keys, values, nd, nd, nd_left, nd_left, nd_right, nd_right, stats, s_left, s_right
     )
+    blocks = lax.all_to_all(copies(gain_grad, ring), "view", 0, 0, axis_index_groups=along, tiled=True)
+    gain_grad = jnp.sum(tied(blocks, kgrad), axis=0)
     return attended, qgrad, kgrad, vgrad, gain_grad
 
 

time: 99.7 us -> 86.4 us (0.87)
  waiting for transfers between devices: 12.4 us -> 0.73 us
  blocking collectives: 22.9 us -> 11.6 us
  starting transfers between devices: 39 us -> 49.8 us
  local copies, waits for them, and re-layouts: 3.01 us -> 1.85 us
    ppermute x6 -> x8, waiting for transfers between devices: 12.4 us -> 0.02 us  [shifted(): lax.ppermute(array, axis, [(i, (i + by) % count) for i in range(count)])]
    all_to_all x2 -> x1, blocking collectives: 22.9 us -> 11.6 us  [total_over(): lax.all_to_all(blocks, axis, 0, 0, axis_index_groups=groups, tiled=True)]
    ppermute x6 -> x8, starting transfers between devices: 33.5 us -> 42.5 us  [shifted(): lax.ppermute(array, axis, [(i, (i + by) % count) for i in range(count)])]
    all_to_all x0 -> x1, starting transfers between devices: none -> 3.35 us  [on_device(): lax.all_to_all(copies(gain_grad, ring), 'view', 0, 0, axis_index_groups=a...]
    all_to_all x1, starting transfers between devices: 5.47 us -> 3.93 us  [total_over(): lax.all_to_all(blocks, axis, 0, 0, axis_index_groups=groups, tiled=True)]
    unnamed x12 -> x8, local copies, waits for them, and re-layouts: 1.68 us -> 0.59 us
    pallas_call x4 -> x5, Pallas kernels: 19.4 us -> 19.5 us  [the longest x2 8 us: query_side(): call(functools.partial(query_kernel, at * PER_STEP), per_half, [scalars]...]
  transfers between devices with their start and end apart: 7 -> 10, of which waited for: 3 -> 1; matrix products, arithmetic and copies ran while one was open for 1% -> 2% of each run, Pallas kernels for 16% -> 21%
where the time goes in v2:
time: 86.4 us; the launch traced here: 85 us
  starting transfers between devices  49.8 us (58%)
  Pallas kernels  19.5 us (23%)
  blocking collectives  11.6 us (13%)
  local copies, waits for them, and re-layouts  1.85 us (2%)
    ppermute x8, starting transfers between devices, shifted(): lax.ppermute(array, axis, [(i, (i + by) % count) for i in range(count)])  42.5 us
    all_to_all x1, blocking collectives, total_over(): lax.all_to_all(blocks, axis, 0, 0, axis_index_groups=groups, tiled=True)  11.6 us
    pallas_call x2, Pallas kernels, query_side(): call(functools.partial(query_kernel, at * PER_STEP), per_half, [scalars]...  8 us
    pallas_call x1, Pallas kernels, on_device(): call(key_kernel, steps, [scalars] + [block(0)] * 2 + own * 3 + [stat_bloc...  5.8 us
    all_to_all x1, starting transfers between devices, total_over(): lax.all_to_all(blocks, axis, 0, 0, axis_index_groups=groups, tiled=True)  3.93 us
    pallas_call x1, Pallas kernels, on_device(): call(prep_kernel, steps, [block(0, steps, thin), block(0, steps, thin), b...  3.89 us
    all_to_all x1, starting transfers between devices, on_device(): lax.all_to_all(copies(gain_grad, ring), 'view', 0, 0, axis_index_groups=a...  3.35 us
    pallas_call x1, Pallas kernels, on_device(): call(pack_kernel, per_half, [scalars, block(0), block(0)], pl.BlockSpec((...  1.85 us
  transfers between devices with their start and end apart: 10, of which 1 were waited for; matrix products, arithmetic and copies ran while one was open for 2% of the time, Pallas kernels for 21%

profile of v2, /device:TPU:1, one launch (start us, length us, event | category | flops | bytes accessed | tf_op | source)
XLA Modules:
  0.0 85.0 jit_solution(4480919220505406271)
XLA Ops:
  0.6 1.9 %pack_kernel.1 = bf16[1,272,1024]{2,1,0:T(8,128)(2,1)} custom-call(s32[2]{0:T(128)} %bitcast.2, bf16[1,128,2048]{2,1,0:T(8,128)(2,1)} %k_ref.5, bf16[1,128,2048]{2,1,0:T(8,128)(2,1)} %v_ref.5), custom_call_target="tpu_custom_call" | custom-call | bytes 2097152 | tf_op jit(solution)/shard_map/pack_kernel/pallas_call | solution.py:206
  2.5 4.8 %collective-permute-start.1 = (bf16[1,272,1024]{2,1,0:T(8,128)(2,1)}, bf16[1,272,1024]{2,1,0:T(8,128)(2,1)S(1)}, u32[]{:S(2)}, u32[]{:S(2)}) collective-permute-start(bf16[1,272,1024]{2,1,0:T(8,128)(2,1)} %pack_kernel.1), channel_id=1, source_target_pairs={{0,1},{1,2},{2,3},{3,4},{4,5},{5,6},{6,7},{7,8},{8,9},{9,10},{10,1... | collective-permute-start | bytes 1671176 | tf_op jit(solution)/shard_map/ppermute | solution.py:27
  7.3 11.5 %collective-permute-start.3 = (bf16[1,272,1024]{2,1,0:T(8,128)(2,1)}, bf16[1,272,1024]{2,1,0:T(8,128)(2,1)}, u32[]{:S(2)}, u32[]{:S(2)}) collective-permute-start(bf16[1,272,1024]{2,1,0:T(8,128)(2,1)} %pack_kernel.1), channel_id=1, source_target_pairs={{0,63},{1,0},{2,1},{3,2},{4,3},{5,4},{6,5},{7,6},{8,7},{9,8},{10,9... | collective-permute-start | bytes 1671176 | tf_op jit(solution)/shard_map/ppermute | solution.py:27
  18.8 3.9 %prep_kernel.1 = (bf16[1,256,1024]{2,1,0:T(8,128)(2,1)}, bf16[1,256,2048]{2,1,0:T(8,128)(2,1)}) custom-call(bf16[1,128,2048]{2,1,0:T(8,128)(2,1)} %k_ref.5, bf16[1,128,2048]{2,1,0:T(8,128)(2,1)} %v_ref.5, bf16[1,128,2048]{2,1,0:T(8,128)(2,1)} %q_ref.5, bf16[1,128,2048]{2,1,0:T(8,128)(2,1)} %do_ref.5, f32[16,128]{1,0:T(8,128)} %gain_ref.5), custom_call_target="tpu_custom_call" | custom-call | flops 4697620480 | bytes 2097152 | tf_op jit(solution)/shard_map/prep_kernel/pallas_call | solution.py:216
  22.7 1.9 %collective-permute-start = (bf16[1,256,1024]{2,1,0:T(8,128)(2,1)}, bf16[1,256,1024]{2,1,0:T(8,128)(2,1)}, u32[]{:S(2)}, u32[]{:S(2)}) collective-permute-start(bf16[1,256,1024]{2,1,0:T(8,128)(2,1)} %get-tuple-element.19), channel_id=1, source_target_pairs={{0,1},{1,2},{2,3},{3,4},{4,5},{5,6},{6,7},{7,8},{8,9},{9,10},{10,1... | collective-permute-start | bytes 1572872 | tf_op jit(solution)/shard_map/ppermute | solution.py:27
  24.6 6.7 %collective-permute-start.2 = (bf16[1,256,1024]{2,1,0:T(8,128)(2,1)}, bf16[1,256,1024]{2,1,0:T(8,128)(2,1)}, u32[]{:S(2)}, u32[]{:S(2)}) collective-permute-start(bf16[1,256,1024]{2,1,0:T(8,128)(2,1)} %get-tuple-element.19), channel_id=1, source_target_pairs={{0,63},{1,0},{2,1},{3,2},{4,3},{5,4},{6,5},{7,6},{8,7},{9,8},{10,9... | collective-permute-start | bytes 1572872 | tf_op jit(solution)/shard_map/ppermute | solution.py:27
  31.3 1.9 %collective-permute-start.4 = (bf16[1,256,2048]{2,1,0:T(8,128)(2,1)}, bf16[1,256,2048]{2,1,0:T(8,128)(2,1)}, u32[]{:S(2)}, u32[]{:S(2)}) collective-permute-start(bf16[1,256,2048]{2,1,0:T(8,128)(2,1)} %get-tuple-element.18.n_ref.n0_ref.d0_ref), channel_id=1, source_target_pairs={{0,1},{1,2},{2,3},{3,4},{4,5},{5,6},{6,7},{7,8},{8,9},{9,10},{10,1... | collective-permute-start | bytes 3145736 | tf_op jit(solution)/shard_map/ppermute | solution.py:27
  33.3 6.7 %collective-permute-start.5 = (bf16[1,256,2048]{2,1,0:T(8,128)(2,1)}, bf16[1,256,2048]{2,1,0:T(8,128)(2,1)}, u32[]{:S(2)}, u32[]{:S(2)}) collective-permute-start(bf16[1,256,2048]{2,1,0:T(8,128)(2,1)} %get-tuple-element.18.n_ref.n0_ref.d0_ref), channel_id=1, source_target_pairs={{0,63},{1,0},{2,1},{3,2},{4,3},{5,4},{6,5},{7,6},{8,7},{9,8},{10,9... | collective-permute-start | bytes 3145736 | tf_op jit(solution)/shard_map/ppermute | solution.py:27
  40.0 0.0 collective-permute-done.3.k2_ref.v2_ref.m2_ref
  40.0 4.0 %query_kernel.2 = (bf16[1,128,2048]{2,1,0:T(8,128)(2,1)}, bf16[1,128,2048]{2,1,0:T(8,128)(2,1)}, f32[64,128]{1,0:T(8,128)}, f32[1,8,128]{2,1,0:T(8,128)}) custom-call(s32[2]{0:T(128)} %bitcast.6, s32[2]{0:T(128)} %bitcast.3, bf16[1,128,2048]{2,1,0:T(8,128)(2,1)} %q_ref.5, bf16[1,256,2048]{2,1,0:T(8,128)(2,1)} %get-tuple-element.18.n_ref.n0_ref.d0_ref, ...), custom_call_target="tpu_custom_call" | custom-call | flops 100663296000 | bytes 2097152 | tf_op jit(solution)/shard_map/query_kernel/pallas_call | solution.py:237
  44.0 0.0 collective-permute-done.k1_ref.v1_ref
  44.0 4.0 %query_kernel.3 = (bf16[1,128,2048]{2,1,0:T(8,128)(2,1)}, bf16[1,128,2048]{2,1,0:T(8,128)(2,1)}, f32[64,128]{1,0:T(8,128)}, f32[8,16,128]{2,1,0:T(8,128)}) custom-call(s32[2]{0:T(128)} %bitcast.7, s32[2]{0:T(128)} %bitcast.4, bf16[1,128,2048]{2,1,0:T(8,128)(2,1)} %q_ref.5, ...), custom_call_target="tpu_custom_call", output_to_operand_aliasing={{0}: (14, {}), {1}: (15, {}), {2}: (16, {})} | custom-call | flops 100663296000 | bytes 2097152 | tf_op jit(solution)/shard_map/query_kernel/pallas_call | solution.py:237
  48.0 11.6 %all_to_all.15 = f32[8,16,128]{2,1,0:T(8,128)S(1)} all-to-all(f32[8,16,128]{2,1,0:T(8,128)} %get-tuple-element.29), channel_id=1, replica_groups=mesh['dp'=8,'view'=64] {'dp'}, dimensions={0} | all-to-all | bytes 131072 | tf_op jit(solution)/shard_map/all_to_all | solution.py:159
  59.6 0.6 broadcast_in_dim.4
  60.3 3.9 %all-to-all-start.1 = ((f32[8,16,128]{2,1,0:T(8,128)}), f32[8,16,128]{2,1,0:T(8,128)S(1)}, u32[]{:S(2)}, u32[]{:S(2)}) async-start(f32[8,16,128]{2,1,0:T(8,128)} %broadcast_in_dim.4), calls=%async_computation.1 | async-start | bytes 131072 | tf_op jit(solution)/shard_map/all_to_all | solution.py:159
  64.2 1.9 %collective-permute-start.6 = (f32[64,128]{1,0:T(8,128)S(1)}, f32[64,128]{1,0:T(8,128)S(1)}, u32[]{:S(2)}, u32[]{:S(2)}) collective-permute-start(f32[64,128]{1,0:T(8,128)S(1)} %copy-done.2), channel_id=1, source_target_pairs={{0,1},{1,2},{2,3},{3,4},{4,5},{5,6},{6,7},{7,8},{8,9},{9,10},{10,1... | collective-permute-start | bytes 98312 | tf_op jit(solution)/shard_map/ppermute | solution.py:27
  66.2 7.1 %collective-permute-start.7 = (f32[64,128]{1,0:T(8,128)S(1)}, f32[64,128]{1,0:T(8,128)S(1)}, u32[]{:S(2)}, u32[]{:S(2)}) collective-permute-start(f32[64,128]{1,0:T(8,128)S(1)} %copy-done.2), channel_id=1, source_target_pairs={{0,63},{1,0},{2,1},{3,2},{4,3},{5,4},{6,5},{7,6},{8,7},{9,8},{10,9... | collective-permute-start | bytes 98312 | tf_op jit(solution)/shard_map/ppermute | solution.py:27
  73.3 0.6 broadcast_in_dim.5
  73.9 3.3 %all-to-all-start.2 = ((f32[8,16,128]{2,1,0:T(8,128)}), f32[8,16,128]{2,1,0:T(8,128)S(1)}, u32[]{:S(2)}, u32[]{:S(2)}) async-start(f32[8,16,128]{2,1,0:T(8,128)} %broadcast_in_dim.5), calls=%async_computation.2 | async-start | bytes 131072 | tf_op jit(solution)/shard_map/all_to_all | solution.py:285
  77.3 0.5 copy-done
  77.9 0.0 copy-done.1
  77.9 5.8 %key_kernel.1 = (bf16[1,128,2048]{2,1,0:T(8,128)(2,1)}, bf16[1,128,2048]{2,1,0:T(8,128)(2,1)}) custom-call(s32[2]{0:T(128)} %bitcast.5, bf16[1,128,2048]{2,1,0:T(8,128)(2,1)} %k_ref.5, bf16[1,128,2048]{2,1,0:T(8,128)(2,1)} %v_ref.5, bf16[1,256,2048]{2,1,0:T(8,128)(2,1)} %get-tuple-element.18.n_ref.n0_ref.d0_ref, ...), custom_call_target="tpu_custom_call" | custom-call | flops 1006632960 | bytes 2097152 | tf_op jit(solution)/shard_map/key_kernel/pallas_call | solution.py:275
  83.7 0.7 all-to-all-done.2
  84.4 0.6 reduce_sum.29
  (15 shorter events, 0.1 us)
Async XLA Ops:
  2.5 30.8 %collective-permute-start.1 = (bf16[1,272,1024]{2,1,0:T(8,128)(2,1)}, bf16[1,272,1024]{2,1,0:T(8,128)(2,1)S(1)}, u32[]{:S(2)}, u32[]{:S(2)}) collective-permute-start(bf16[1,272,1024]{2,1,0:T(8,128)(2,1)} %pack_kernel.1), channel_id=1, source_target_pairs={{0,1},{1,2},{2,3},{3,4},{4,5},{5,6},{6,7},{7,8},{8,9},{9,10},{10,1... | collective-permute-start | bytes 1671176 | tf_op jit(solution)/shard_map/ppermute | solution.py:27
  7.3 32.6 %collective-permute-start.3 = (bf16[1,272,1024]{2,1,0:T(8,128)(2,1)}, bf16[1,272,1024]{2,1,0:T(8,128)(2,1)}, u32[]{:S(2)}, u32[]{:S(2)}) collective-permute-start(bf16[1,272,1024]{2,1,0:T(8,128)(2,1)} %pack_kernel.1), channel_id=1, source_target_pairs={{0,63},{1,0},{2,1},{3,2},{4,3},{5,4},{6,5},{7,6},{8,7},{9,8},{10,9... | collective-permute-start | bytes 1671176 | tf_op jit(solution)/shard_map/ppermute | solution.py:27
  22.7 21.3 %collective-permute-start = (bf16[1,256,1024]{2,1,0:T(8,128)(2,1)}, bf16[1,256,1024]{2,1,0:T(8,128)(2,1)}, u32[]{:S(2)}, u32[]{:S(2)}) collective-permute-start(bf16[1,256,1024]{2,1,0:T(8,128)(2,1)} %get-tuple-element.19), channel_id=1, source_target_pairs={{0,1},{1,2},{2,3},{3,4},{4,5},{5,6},{6,7},{7,8},{8,9},{9,10},{10,1... | collective-permute-start | bytes 1572872 | tf_op jit(solution)/shard_map/ppermute | solution.py:27
  24.6 19.4 %collective-permute-start.2 = (bf16[1,256,1024]{2,1,0:T(8,128)(2,1)}, bf16[1,256,1024]{2,1,0:T(8,128)(2,1)}, u32[]{:S(2)}, u32[]{:S(2)}) collective-permute-start(bf16[1,256,1024]{2,1,0:T(8,128)(2,1)} %get-tuple-element.19), channel_id=1, source_target_pairs={{0,63},{1,0},{2,1},{3,2},{4,3},{5,4},{6,5},{7,6},{8,7},{9,8},{10,9... | collective-permute-start | bytes 1572872 | tf_op jit(solution)/shard_map/ppermute | solution.py:27
  31.3 46.0 %collective-permute-start.4 = (bf16[1,256,2048]{2,1,0:T(8,128)(2,1)}, bf16[1,256,2048]{2,1,0:T(8,128)(2,1)}, u32[]{:S(2)}, u32[]{:S(2)}) collective-permute-start(bf16[1,256,2048]{2,1,0:T(8,128)(2,1)} %get-tuple-element.18.n_ref.n0_ref.d0_ref), channel_id=1, source_target_pairs={{0,1},{1,2},{2,3},{3,4},{4,5},{5,6},{6,7},{7,8},{8,9},{9,10},{10,1... | collective-permute-start | bytes 3145736 | tf_op jit(solution)/shard_map/ppermute | solution.py:27
  33.2 6.7 %copy-start.3 = (bf16[1,272,1024]{2,1,0:T(8,128)(2,1)}, bf16[1,272,1024]{2,1,0:T(8,128)(2,1)S(1)}, u32[]{:S(2)}) copy-start(bf16[1,272,1024]{2,1,0:T(8,128)(2,1)S(1)} %collective-permute-done.1.k1_ref.v1_ref.m1_ref) | copy-start | bytes 1671172
  33.3 44.1 %collective-permute-start.5 = (bf16[1,256,2048]{2,1,0:T(8,128)(2,1)}, bf16[1,256,2048]{2,1,0:T(8,128)(2,1)}, u32[]{:S(2)}, u32[]{:S(2)}) collective-permute-start(bf16[1,256,2048]{2,1,0:T(8,128)(2,1)} %get-tuple-element.18.n_ref.n0_ref.d0_ref), channel_id=1, source_target_pairs={{0,63},{1,0},{2,1},{3,2},{4,3},{5,4},{6,5},{7,6},{8,7},{9,8},{10,9... | collective-permute-start | bytes 3145736 | tf_op jit(solution)/shard_map/ppermute | solution.py:27
  60.3 3.9 %copy-start.2 = (f32[64,128]{1,0:T(8,128)S(1)}, f32[64,128]{1,0:T(8,128)}, u32[]{:S(2)}) copy-start(f32[64,128]{1,0:T(8,128)} %get-tuple-element.26.s0_ref) | copy-start | bytes 98308
  60.3 13.0 %all-to-all-start.1 = ((f32[8,16,128]{2,1,0:T(8,128)}), f32[8,16,128]{2,1,0:T(8,128)S(1)}, u32[]{:S(2)}, u32[]{:S(2)}) async-start(f32[8,16,128]{2,1,0:T(8,128)} %broadcast_in_dim.4), calls=%async_computation.1 | async-start | bytes 131072 | tf_op jit(solution)/shard_map/all_to_all | solution.py:159
  64.2 13.1 %collective-permute-start.6 = (f32[64,128]{1,0:T(8,128)S(1)}, f32[64,128]{1,0:T(8,128)S(1)}, u32[]{:S(2)}, u32[]{:S(2)}) collective-permute-start(f32[64,128]{1,0:T(8,128)S(1)} %copy-done.2), channel_id=1, source_target_pairs={{0,1},{1,2},{2,3},{3,4},{4,5},{5,6},{6,7},{7,8},{8,9},{9,10},{10,1... | collective-permute-start | bytes 98312 | tf_op jit(solution)/shard_map/ppermute | solution.py:27
  66.2 11.2 %collective-permute-start.7 = (f32[64,128]{1,0:T(8,128)S(1)}, f32[64,128]{1,0:T(8,128)S(1)}, u32[]{:S(2)}, u32[]{:S(2)}) collective-permute-start(f32[64,128]{1,0:T(8,128)S(1)} %copy-done.2), channel_id=1, source_target_pairs={{0,63},{1,0},{2,1},{3,2},{4,3},{5,4},{6,5},{7,6},{8,7},{9,8},{10,9... | collective-permute-start | bytes 98312 | tf_op jit(solution)/shard_map/ppermute | solution.py:27
  73.9 10.5 %all-to-all-start.2 = ((f32[8,16,128]{2,1,0:T(8,128)}), f32[8,16,128]{2,1,0:T(8,128)S(1)}, u32[]{:S(2)}, u32[]{:S(2)}) async-start(f32[8,16,128]{2,1,0:T(8,128)} %broadcast_in_dim.5), calls=%async_computation.2 | async-start | bytes 131072 | tf_op jit(solution)/shard_map/all_to_all | solution.py:285
  77.3 0.6 copy-start
  77.3 0.6 copy-start.1

commit v3 on v2

--- a/solution.py
+++ b/solution.py
@@ -13,6 +13,8 @@
 PER_STEP = 4
 STATS = 4
 MASK_ROWS = 16
+PREP_STEPS = 2
+SHARE = 2
 RING = 8
 NT = (((1,), (1,)), ((), ()))
 NN = (((1,), (0,)), ((), ()))
@@ -43,7 +45,7 @@
     strip, width = k_ref.shape[1:]
     out_ref[0, :strip, :] = k_ref[0]
     out_ref[0, strip : 2 * strip, :] = v_ref[0]
-    at = lax.broadcasted_iota(jnp.int32, (MASK_ROWS, width), 1)
+    at = lax.broadcasted_iota(jnp.int32, (MASK_ROWS, width), 1) % strip
     valid = (at >= own_ref[0]) & (at < own_ref[1])
     out_ref[0, 2 * strip :, :] = valid.astype(jnp.float32).astype(jnp.bfloat16)
 
@@ -53,9 +55,10 @@
     strip = k_ref.shape[1]
     kv_ref[0, :strip, :] = k_ref[0]
     kv_ref[0, strip:, :] = v_ref[0]
-    for i in range(PER_STEP):
+    count = q_ref.shape[2] // HEAD_DIM
+    for i in range(count):
         q = head(q_ref, i).astype(jnp.float32)
-        gain = gain_ref[pl.ds(step * PER_STEP + i, 1), :]
+        gain = gain_ref[pl.ds(step * count + i, 1), :]
         scale = lax.rsqrt(jnp.mean(q * q, axis=-1, keepdims=True) + EPS)
         nd_ref[0, :strip, columns_of(i)] = (q * scale * gain).astype(jnp.bfloat16)
     nd_ref[0, strip:, :] = do_ref[0]
@@ -132,7 +135,7 @@
         [jnp.broadcast_to(valid, (strip, strip)), valid & left, valid & right], axis=1
     )
     normed, dout = (n0_ref, n1_ref, n2_ref), (d0_ref, d1_ref, d2_ref)
-    each = range(PER_STEP)
+    each = range(2 * PER_STEP)
     scores = [dot(head(k_ref, i), heads_of(normed, i), NT) for i in each]
     dprob = [dot(head(v_ref, i), heads_of(dout, i), NT) for i in each]
     prob_b, dscore = [], []
@@ -173,8 +176,10 @@
     heads = width // HEAD_DIM
     steps = heads // PER_STEP
     cols = PER_STEP * HEAD_DIM
-    halves = 2
-    per_half = steps // halves
+    late_steps = max(steps // SHARE, 1)
+    early_steps = steps - late_steps
+    early_heads, late_width = early_steps * PER_STEP, late_steps * cols
+    early_width = width - late_width
     n_dp = lax.axis_size("dp")
     count = lax.axis_size("view")
     ring = RING if count % RING == 0 else count
@@ -190,7 +195,7 @@
     mac = strip * strip * width
 
     def call(kernel, grid, in_specs, out_specs, out_shape, cost=0, aliases=None):
-        return pl.pallas_call(
+        run = pl.pallas_call(
             kernel,
             grid=(grid,),
             in_specs=in_specs,
@@ -198,48 +203,54 @@
             out_shape=out_shape,
             input_output_aliases=aliases or {},
             name=(kernel.func if isinstance(kernel, functools.partial) else kernel).__name__,
-            compiler_params=pltpu.CompilerParams(vmem_limit_bytes=63 * 1024 * 1024),
+            compiler_params=pltpu.CompilerParams(vmem_limit_bytes=(63 if kernel is pack_kernel else 40) * 1024 * 1024),
             cost_estimate=pl.CostEstimate(flops=cost * mac, bytes_accessed=8 * strip * width, transcendentals=0),
         )
+        return lambda *args: run(
+            *(pltpu.with_memory_space_constraint(a, pltpu.VMEM) if kernel is key_kernel and a.size > 1 << 12 else a for a in args)
+        )
 
     rows = 2 * strip + MASK_ROWS
+    parts = PREP_STEPS
+    thin, slim, part = early_width // parts, late_width // parts, width // parts
     kv0 = call(
         pack_kernel,
-        per_half,
-        [scalars, block(0), block(0)],
-        pl.BlockSpec((1, rows, cols), lambda i: (0, 0, i)),
-        jax.ShapeDtypeStruct((1, rows, width // halves), jnp.bfloat16),
+        parts,
+        [scalars, block(0, 0, thin), block(0, 0, thin)],
+        pl.BlockSpec((1, rows, thin), lambda i: (0, 0, i)),
+        jax.ShapeDtypeStruct((1, rows, early_width), jnp.bfloat16),
     )(own_bounds, keys, values)
     kv0_left, kv0_right = shifted(kv0, "view", 1), shifted(kv0, "view", -1)
-
-    thin = cols // halves
+    late = block(0, early_width // slim, slim)
     kv1, nd = call(
         prep_kernel,
-        steps,
-        [block(0, steps, thin), block(0, steps, thin), block(0), block(0), whole],
+        parts,
+        [late, late, block(0, 0, part), block(0, 0, part), whole],
         [
-            pl.BlockSpec((1, 2 * strip, thin), lambda i: (0, 0, i)),
-            pl.BlockSpec((1, 2 * strip, cols), lambda i: (0, 0, i)),
+            pl.BlockSpec((1, 2 * strip, slim), lambda i: (0, 0, i)),
+            pl.BlockSpec((1, 2 * strip, part), lambda i: (0, 0, i)),
         ],
         [
-            jax.ShapeDtypeStruct((1, 2 * strip, width // halves), jnp.bfloat16),
+            jax.ShapeDtypeStruct((1, 2 * strip, late_width), jnp.bfloat16),
             jax.ShapeDtypeStruct((1, 2 * strip, width), jnp.bfloat16),
         ],
         cost=140,
     )(keys, values, queries, out_grad, gain)
+
     kv1_left, kv1_right = shifted(kv1, "view", 1), shifted(kv1, "view", -1)
 
     def query_side(half, left, right, before):
-        at = half * per_half
+        near_args = [left, left, kv0_left, right, right, kv0_right]
+        at = early_steps if half else 0
         mask = pl.BlockSpec((1, MASK_ROWS, strip), lambda i: (0, 2 * strip // MASK_ROWS, 0))
         near = [block(0), block(1), mask]
-        count, per = (1, heads // halves) if half == 0 else (n_dp, heads)
+        count, per = (n_dp, heads) if half else (1, early_heads)
         return call(
             functools.partial(query_kernel, at * PER_STEP),
-            per_half,
+            late_steps if half else early_steps,
             [scalars] * 2 + [block(0, at)] * 5 + near * 2 + [whole]
             + [anywhere] * (3 if half else 0)
-            + [pl.BlockSpec((1, heads // halves, HEAD_DIM), lambda i: (0, 0, 0))] * (1 if half else 0),
+            + [pl.BlockSpec((1, early_heads, HEAD_DIM), lambda i: (0, 0, 0))] * (1 if half else 0),
             [
                 block(0, at),
                 block(0, at),
@@ -256,13 +267,15 @@
             aliases={14: 0, 15: 1, 16: 2} if half else None,
         )(
             own_tasks, own_bounds, queries, nd, out_grad, keys, values,
-            left, left, kv0_left, right, right, kv0_right, gain, *before,
-        )
-
+            *near_args, gain, *before,
+        )
+
+    kv0_right, kv0_left = lax.optimization_barrier((kv0_right, kv0_left))
     early = query_side(0, kv0_left, kv0_right, ())
     attended, qgrad, stats, gain_parts = query_side(1, kv1_left, kv1_right, early)
-    nd_sent = nd
+    nd_sent = tied(nd, early[3])
     nd_left, nd_right = shifted(nd_sent, "view", 1), shifted(nd_sent, "view", -1)
+    nd_right, nd_left = lax.optimization_barrier((nd_right, nd_left))
     s_left, s_right = shifted(stats, "view", 1), shifted(stats, "view", -1)
 
     across = [[y * ring + z for y in range(count // ring)] for z in range(ring)]
@@ -270,13 +283,14 @@
     gain_grad = total_over(gain_parts, "dp")
     gain_grad = total_over(copies(gain_grad, count // ring), "view", across)
 
-    own = [block(0), block(1)]
-    stat_block = pl.BlockSpec((PER_STEP * STATS, strip), lambda i: (i, 0))
+    both = 2 * cols
+    own = [block(0, 0, both), block(1, 0, both)]
+    stat_block = pl.BlockSpec((2 * PER_STEP * STATS, strip), lambda i: (i, 0))
     kgrad, vgrad = call(
         key_kernel,
-        steps,
-        [scalars] + [block(0)] * 2 + own * 3 + [stat_block] * 3,
-        [block(0)] * 2,
+        steps // 2,
+        [scalars] + [block(0, 0, both)] * 2 + own * 3 + [stat_block] * 3,
+        [block(0, 0, both)] * 2,
         [wide, wide],
         cost=30,
     )(

time: 86.4 us -> 85.2 us (0.986)
  starting transfers between devices: 49.8 us -> 44 us
  Pallas kernels: 19.5 us -> 13.8 us
  local copies, waits for them, and re-layouts: 1.85 us -> 7.14 us
  waiting for transfers between devices: 0.73 us -> 4.4 us
  blocking collectives: 11.6 us -> 13.3 us
    ppermute x8, starting transfers between devices: 42.5 us -> 36.8 us  [shifted(): lax.ppermute(array, axis, [(i, (i + by) % count) for i in range(count)])]
    pallas_call x5, Pallas kernels: 19.5 us -> 13.8 us  [call(): run(*(pltpu.with_memory_space_constraint(a, pltpu.VMEM) if kernel is key_...]
    unnamed x8 -> x26, local copies, waits for them, and re-layouts: 0.59 us -> 5.89 us
    ppermute x8, waiting for transfers between devices: 0.02 us -> 3.19 us  [shifted(): lax.ppermute(array, axis, [(i, (i + by) % count) for i in range(count)])]
    all_to_all x1, blocking collectives: 11.6 us -> 13.3 us  [total_over(): lax.all_to_all(blocks, axis, 0, 0, axis_index_groups=groups, tiled=True)]
    all_to_all x1, waiting for transfers between devices: 0.01 us -> 1.21 us  [total_over(): lax.all_to_all(blocks, axis, 0, 0, axis_index_groups=groups, tiled=True)]
  transfers between devices with their start and end apart: 10 -> 10, of which waited for: 1 -> 4; matrix products, arithmetic and copies ran while one was open for 2% -> 2% of each run, Pallas kernels for 21% -> 14%
where the time goes in v3:
time: 85.2 us; the launch traced here: 84.1 us
  starting transfers between devices  44 us (52%)
  Pallas kernels  13.8 us (16%)
  blocking collectives  13.3 us (16%)
  local copies, waits for them, and re-layouts  7.14 us (8%)
  waiting for transfers between devices  4.4 us (5%)
    ppermute x8, starting transfers between devices, shifted(): lax.ppermute(array, axis, [(i, (i + by) % count) for i in range(count)])  36.8 us
    pallas_call x5, Pallas kernels, call(): run(*(pltpu.with_memory_space_constraint(a, pltpu.VMEM) if kernel is key_...  13.8 us
    all_to_all x1, blocking collectives, total_over(): lax.all_to_all(blocks, axis, 0, 0, axis_index_groups=groups, tiled=True)  13.3 us
    unnamed x26, local copies, waits for them, and re-layouts  5.89 us
    all_to_all x1, starting transfers between devices, total_over(): lax.all_to_all(blocks, axis, 0, 0, axis_index_groups=groups, tiled=True)  3.8 us
    all_to_all x1, starting transfers between devices, on_device(): lax.all_to_all(copies(gain_grad, ring), 'view', 0, 0, axis_index_groups=a...  3.35 us
    ppermute x8, waiting for transfers between devices, shifted(): lax.ppermute(array, axis, [(i, (i + by) % count) for i in range(count)])  3.19 us
  transfers between devices with their start and end apart: 10, of which 4 were waited for; matrix products, arithmetic and copies ran while one was open for 2% of the time, Pallas kernels for 14%

profile of v3, /device:TPU:1, one launch (start us, length us, event | category | flops | bytes accessed | tf_op | source)
XLA Modules:
  0.0 84.1 jit_solution(16268205129425384951)
XLA Ops:
  0.7 1.9 %pack_kernel.1 = bf16[1,272,1024]{2,1,0:T(8,128)(2,1)} custom-call(s32[2]{0:T(128)} %bitcast.2, bf16[1,128,2048]{2,1,0:T(8,128)(2,1)} %k_ref.5, bf16[1,128,2048]{2,1,0:T(8,128)(2,1)} %v_ref.5), custom_call_target="tpu_custom_call" | custom-call | bytes 2097152 | tf_op jit(solution)/shard_map/pack_kernel/pallas_call | solution.py:209
  2.6 4.8 %collective-permute-start.2 = (bf16[1,272,1024]{2,1,0:T(8,128)(2,1)}, bf16[1,272,1024]{2,1,0:T(8,128)(2,1)S(1)}, u32[]{:S(2)}, u32[]{:S(2)}) collective-permute-start(bf16[1,272,1024]{2,1,0:T(8,128)(2,1)} %pack_kernel.1), channel_id=1, source_target_pairs={{0,1},{1,2},{2,3},{3,4},{4,5},{5,6},{6,7},{7,8},{8,9},{9,10},{10,1... | collective-permute-start | bytes 1671176 | tf_op jit(solution)/shard_map/ppermute | solution.py:29
  7.4 11.5 %collective-permute-start.1 = (bf16[1,272,1024]{2,1,0:T(8,128)(2,1)}, bf16[1,272,1024]{2,1,0:T(8,128)(2,1)S(1)}, u32[]{:S(2)}, u32[]{:S(2)}) collective-permute-start(bf16[1,272,1024]{2,1,0:T(8,128)(2,1)} %pack_kernel.1), channel_id=1, source_target_pairs={{0,63},{1,0},{2,1},{3,2},{4,3},{5,4},{6,5},{7,6},{8,7},{9,8},{10,9... | collective-permute-start | bytes 1671176 | tf_op jit(solution)/shard_map/ppermute | solution.py:29
  18.9 1.0 %copy-done.3 = bf16[1,128,2048]{2,1,0:T(8,128)(2,1)S(1)} copy-done((bf16[1,128,2048]{2,1,0:T(8,128)(2,1)S(1)}, bf16[1,128,2048]{2,1,0:T(8,128)(2,1)}, u32[]{:S(2)}) %copy-start.3) | copy-done | bytes 524312
  20.0 1.0 %copy-done.7 = bf16[1,128,2048]{2,1,0:T(8,128)(2,1)S(1)} copy-done((bf16[1,128,2048]{2,1,0:T(8,128)(2,1)S(1)}, bf16[1,128,2048]{2,1,0:T(8,128)(2,1)}, u32[]{:S(2)}) %copy-start.7) | copy-done | bytes 524312
  21.0 1.0 %copy-done.9 = bf16[1,128,2048]{2,1,0:T(8,128)(2,1)S(1)} copy-done((bf16[1,128,2048]{2,1,0:T(8,128)(2,1)S(1)}, bf16[1,128,2048]{2,1,0:T(8,128)(2,1)}, u32[]{:S(2)}) %copy-start.9) | copy-done | bytes 524312
  22.8 3.4 %collective-permute-start.3 = (bf16[1,256,1024]{2,1,0:T(8,128)(2,1)S(1)}, bf16[1,256,1024]{2,1,0:T(8,128)(2,1)S(1)}, u32[]{:S(2)}, u32[]{:S(2)}) collective-permute-start(bf16[1,256,1024]{2,1,0:T(8,128)(2,1)S(1)} %get-tuple-element.24), channel_id=1, source_target_pairs={{0,63},{1,0},{2,1},{3,2},{4,3},{5,4},{6,5},{7,6},{8,7},{9,8},{10,9... | collective-permute-start | bytes 1572872 | tf_op jit(solution)/shard_map/ppermute | solution.py:29
  26.2 1.9 %collective-permute-start = (bf16[1,256,1024]{2,1,0:T(8,128)(2,1)S(1)}, bf16[1,256,1024]{2,1,0:T(8,128)(2,1)S(1)}, u32[]{:S(2)}, u32[]{:S(2)}) collective-permute-start(bf16[1,256,1024]{2,1,0:T(8,128)(2,1)S(1)} %get-tuple-element.24), channel_id=1, source_target_pairs={{0,1},{1,2},{2,3},{3,4},{4,5},{5,6},{6,7},{7,8},{8,9},{9,10},{10,1... | collective-permute-start | bytes 1572872 | tf_op jit(solution)/shard_map/ppermute | solution.py:29
  28.1 1.4 %collective-permute-done.2.k1_ref.v1_ref.m1_ref = bf16[1,272,1024]{2,1,0:T(8,128)(2,1)S(1)} collective-permute-done((bf16[1,272,1024]{2,1,0:T(8,128)(2,1)}, bf16[1,272,1024]{2,1,0:T(8,128)(2,1)S(1)}, u32[]{:S(2)}, u32[]{:S(2)}) %collective-permute-start.2) | collective-permute-done | bytes 557088 | tf_op jit(solution)/shard_map/ppermute | solution.py:29
  29.5 1.0 %collective-permute-done.1.k2_ref.v2_ref.m2_ref = bf16[1,272,1024]{2,1,0:T(8,128)(2,1)S(1)} collective-permute-done((bf16[1,272,1024]{2,1,0:T(8,128)(2,1)}, bf16[1,272,1024]{2,1,0:T(8,128)(2,1)S(1)}, u32[]{:S(2)}, u32[]{:S(2)}) %collective-permute-start.1) | collective-permute-done | bytes 557088 | tf_op jit(solution)/shard_map/ppermute | solution.py:29
  31.2 3.3 %query_kernel.2 = (bf16[1,128,2048]{2,1,0:T(8,128)(2,1)}, bf16[1,128,2048]{2,1,0:T(8,128)(2,1)}, f32[64,128]{1,0:T(8,128)S(1)}, f32[1,8,128]{2,1,0:T(8,128)S(1)}) custom-call(s32[2]{0:T(128)S(1)} %bitcast.6, s32[2]{0:T(128)S(1)} %bitcast.3, bf16[1,128,2048]{2,1,0:T(8,128)(2,1)S(1)} %copy-done.7, ...), custom_call_target="tpu_custom_call" | custom-call | flops 100663296000 | bytes 2097152 | tf_op jit(solution)/shard_map/query_kernel/pallas_call | solution.py:209
  34.4 1.9 %collective-permute-start.5 = (bf16[1,256,2048]{2,1,0:T(8,128)(2,1)S(1)}, bf16[1,256,2048]{2,1,0:T(8,128)(2,1)S(1)}, u32[]{:S(2)}, u32[]{:S(2)}) collective-permute-start(bf16[1,256,2048]{2,1,0:T(8,128)(2,1)S(1)} %get-tuple-element.33.n_ref.n0_ref.d0_ref), channel_id=1, source_target_pairs={{0,1},{1,2},{2,3},{3,4},{4,5},{5,6},{6,7},{7,8},{8,9},{9,10},{10,1... | collective-permute-start | bytes 3145736 | tf_op jit(solution)/shard_map/ppermute | solution.py:29
  36.4 7.3 %collective-permute-start.4 = (bf16[1,256,2048]{2,1,0:T(8,128)(2,1)S(1)}, bf16[1,256,2048]{2,1,0:T(8,128)(2,1)S(1)}, u32[]{:S(2)}, u32[]{:S(2)}) collective-permute-start(bf16[1,256,2048]{2,1,0:T(8,128)(2,1)S(1)} %get-tuple-element.33.n_ref.n0_ref.d0_ref), channel_id=1, source_target_pairs={{0,63},{1,0},{2,1},{3,2},{4,3},{5,4},{6,5},{7,6},{8,7},{9,8},{10,9... | collective-permute-start | bytes 3145736 | tf_op jit(solution)/shard_map/ppermute | solution.py:29
  43.7 3.3 %query_kernel.3 = (bf16[1,128,2048]{2,1,0:T(8,128)(2,1)}, bf16[1,128,2048]{2,1,0:T(8,128)(2,1)}, f32[64,128]{1,0:T(8,128)S(1)}, f32[8,16,128]{2,1,0:T(8,128)S(1)}) custom-call(s32[2]{0:T(128)S(1)} %bitcast.7, s32[2]{0:T(128)S(1)} %bitcast.4, bf16[1,128,2048]{2,1,0:T(8,128)(2,1)S(1)} %copy-done.8, ...), custom_call_target="tpu_custom_call", output_to_operand_aliasing={{0}: (14, {}), {1}: (15, {}), {2}: (16, {})} | custom-call | flops 100663296000 | bytes 2097152 | tf_op jit(solution)/shard_map/query_kernel/pallas_call | solution.py:209
  47.0 13.3 %all_to_all.15 = f32[8,16,128]{2,1,0:T(8,128)S(1)} all-to-all(f32[8,16,128]{2,1,0:T(8,128)S(1)} %get-tuple-element.39), channel_id=1, replica_groups=mesh['dp'=8,'view'=64] {'dp'}, dimensions={0} | all-to-all | bytes 131072 | tf_op jit(solution)/shard_map/all_to_all | solution.py:162
  61.0 3.8 %all-to-all-start.1 = ((f32[8,16,128]{2,1,0:T(8,128)}), f32[8,16,128]{2,1,0:T(8,128)S(1)}, u32[]{:S(2)}, u32[]{:S(2)}) async-start(f32[8,16,128]{2,1,0:T(8,128)} %broadcast_in_dim.4), calls=%async_computation.1 | async-start | bytes 131072 | tf_op jit(solution)/shard_map/all_to_all | solution.py:162
  64.8 4.1 %collective-permute-start.7 = (f32[64,128]{1,0:T(8,128)S(1)}, f32[64,128]{1,0:T(8,128)S(1)}, u32[]{:S(2)}, u32[]{:S(2)}) collective-permute-start(f32[64,128]{1,0:T(8,128)S(1)} %get-tuple-element.36.s0_ref), channel_id=1, source_target_pairs={{0,63},{1,0},{2,1},{3,2},{4,3},{5,4},{6,5},{7,6},{8,7},{9,8},{10,9... | collective-permute-start | bytes 98312 | tf_op jit(solution)/shard_map/ppermute | solution.py:29
  68.9 1.9 %collective-permute-start.6 = (f32[64,128]{1,0:T(8,128)S(1)}, f32[64,128]{1,0:T(8,128)S(1)}, u32[]{:S(2)}, u32[]{:S(2)}) collective-permute-start(f32[64,128]{1,0:T(8,128)S(1)} %get-tuple-element.36.s0_ref), channel_id=1, source_target_pairs={{0,1},{1,2},{2,3},{3,4},{4,5},{5,6},{6,7},{7,8},{8,9},{9,10},{10,1... | collective-permute-start | bytes 98312 | tf_op jit(solution)/shard_map/ppermute | solution.py:29
  70.8 1.2 %all-to-all-done.1 = f32[8,16,128]{2,1,0:T(8,128)S(1)} async-done(((f32[8,16,128]{2,1,0:T(8,128)}), f32[8,16,128]{2,1,0:T(8,128)S(1)}, u32[]{:S(2)}, u32[]{:S(2)}) %all-to-all-start.1) | async-done | bytes 65568 | tf_op jit(solution)/shard_map/all_to_all | solution.py:162
  72.7 3.3 %all-to-all-start.2 = ((f32[8,16,128]{2,1,0:T(8,128)}), f32[8,16,128]{2,1,0:T(8,128)S(1)}, u32[]{:S(2)}, u32[]{:S(2)}) async-start(f32[8,16,128]{2,1,0:T(8,128)} %broadcast_in_dim.5), calls=%async_computation.2 | async-start | bytes 131072 | tf_op jit(solution)/shard_map/all_to_all | solution.py:299
  76.1 0.8 collective-permute-done.6.s1_ref
  76.9 1.0 %copy-done.2 = bf16[1,128,2048]{2,1,0:T(8,128)(2,1)S(1)} copy-done((bf16[1,128,2048]{2,1,0:T(8,128)(2,1)S(1)}, bf16[1,128,2048]{2,1,0:T(8,128)(2,1)}, u32[]{:S(2)}) %copy-start.2) | copy-done | bytes 524312
  77.9 1.0 %copy-done.5 = bf16[1,128,2048]{2,1,0:T(8,128)(2,1)S(1)} copy-done((bf16[1,128,2048]{2,1,0:T(8,128)(2,1)S(1)}, bf16[1,128,2048]{2,1,0:T(8,128)(2,1)}, u32[]{:S(2)}) %copy-start.5) | copy-done | bytes 524312
  79.0 4.6 %key_kernel.1 = (bf16[1,128,2048]{2,1,0:T(8,128)(2,1)}, bf16[1,128,2048]{2,1,0:T(8,128)(2,1)}) custom-call(s32[2]{0:T(128)S(1)} %bitcast.5, bf16[1,128,2048]{2,1,0:T(8,128)(2,1)S(1)} %copy-done.2, bf16[1,128,2048]{2,1,0:T(8,128)(2,1)S(1)} %copy-done.5, bf16[1,256,2048]{2,1,0:T(8,128)(2,1)S(1)} %get-tuple-element.33.n_ref.n0_ref.d0_ref, ...), custom_call_target="tpu_custom_call" | custom-call | flops 1006632960 | bytes 2097152 | tf_op jit(solution)/shard_map/key_kernel/pallas_call | solution.py:209
  (33 shorter events, 3.4 us)
Async XLA Ops:
  0.6 18.3 %copy-start = (bf16[1,128,2048]{2,1,0:T(8,128)(2,1)S(1)}, bf16[1,128,2048]{2,1,0:T(8,128)(2,1)}, u32[]{:S(2)}) copy-start(bf16[1,128,2048]{2,1,0:T(8,128)(2,1)} %k_ref.5) | copy-start | bytes 1572868
  0.6 18.3 %copy-start.11 = (f32[16,128]{1,0:T(8,128)S(1)}, f32[16,128]{1,0:T(8,128)}, u32[]{:S(2)}) copy-start(f32[16,128]{1,0:T(8,128)} %gain_ref.5) | copy-start | bytes 24580
  2.6 26.9 %collective-permute-start.2 = (bf16[1,272,1024]{2,1,0:T(8,128)(2,1)}, bf16[1,272,1024]{2,1,0:T(8,128)(2,1)S(1)}, u32[]{:S(2)}, u32[]{:S(2)}) collective-permute-start(bf16[1,272,1024]{2,1,0:T(8,128)(2,1)} %pack_kernel.1), channel_id=1, source_target_pairs={{0,1},{1,2},{2,3},{3,4},{4,5},{5,6},{6,7},{7,8},{8,9},{9,10},{10,1... | collective-permute-start | bytes 1671176 | tf_op jit(solution)/shard_map/ppermute | solution.py:29
  7.4 23.1 %collective-permute-start.1 = (bf16[1,272,1024]{2,1,0:T(8,128)(2,1)}, bf16[1,272,1024]{2,1,0:T(8,128)(2,1)S(1)}, u32[]{:S(2)}, u32[]{:S(2)}) collective-permute-start(bf16[1,272,1024]{2,1,0:T(8,128)(2,1)} %pack_kernel.1), channel_id=1, source_target_pairs={{0,63},{1,0},{2,1},{3,2},{4,3},{5,4},{6,5},{7,6},{8,7},{9,8},{10,9... | collective-permute-start | bytes 1671176 | tf_op jit(solution)/shard_map/ppermute | solution.py:29
  18.9 1.0 %copy-start.3 = (bf16[1,128,2048]{2,1,0:T(8,128)(2,1)S(1)}, bf16[1,128,2048]{2,1,0:T(8,128)(2,1)}, u32[]{:S(2)}) copy-start(bf16[1,128,2048]{2,1,0:T(8,128)(2,1)} %v_ref.5) | copy-start | bytes 1572868
  20.0 1.0 %copy-start.7 = (bf16[1,128,2048]{2,1,0:T(8,128)(2,1)S(1)}, bf16[1,128,2048]{2,1,0:T(8,128)(2,1)}, u32[]{:S(2)}) copy-start(bf16[1,128,2048]{2,1,0:T(8,128)(2,1)} %q_ref.5) | copy-start | bytes 1572868
  21.0 1.0 %copy-start.9 = (bf16[1,128,2048]{2,1,0:T(8,128)(2,1)S(1)}, bf16[1,128,2048]{2,1,0:T(8,128)(2,1)}, u32[]{:S(2)}) copy-start(bf16[1,128,2048]{2,1,0:T(8,128)(2,1)} %do_ref.5) | copy-start | bytes 1572868
  22.1 8.4 %copy-start.4 = (bf16[1,128,2048]{2,1,0:T(8,128)(2,1)S(1)}, bf16[1,128,2048]{2,1,0:T(8,128)(2,1)}, u32[]{:S(2)}) copy-start(bf16[1,128,2048]{2,1,0:T(8,128)(2,1)} %v_ref.5) | copy-start | bytes 1572868
  22.1 8.4 %copy-start.10 = (bf16[1,128,2048]{2,1,0:T(8,128)(2,1)S(1)}, bf16[1,128,2048]{2,1,0:T(8,128)(2,1)}, u32[]{:S(2)}) copy-start(bf16[1,128,2048]{2,1,0:T(8,128)(2,1)} %do_ref.5) | copy-start | bytes 1572868
  22.8 20.9 %collective-permute-start.3 = (bf16[1,256,1024]{2,1,0:T(8,128)(2,1)S(1)}, bf16[1,256,1024]{2,1,0:T(8,128)(2,1)S(1)}, u32[]{:S(2)}, u32[]{:S(2)}) collective-permute-start(bf16[1,256,1024]{2,1,0:T(8,128)(2,1)S(1)} %get-tuple-element.24), channel_id=1, source_target_pairs={{0,63},{1,0},{2,1},{3,2},{4,3},{5,4},{6,5},{7,6},{8,7},{9,8},{10,9... | collective-permute-start | bytes 1572872 | tf_op jit(solution)/shard_map/ppermute | solution.py:29
  26.2 17.5 %collective-permute-start = (bf16[1,256,1024]{2,1,0:T(8,128)(2,1)S(1)}, bf16[1,256,1024]{2,1,0:T(8,128)(2,1)S(1)}, u32[]{:S(2)}, u32[]{:S(2)}) collective-permute-start(bf16[1,256,1024]{2,1,0:T(8,128)(2,1)S(1)} %get-tuple-element.24), channel_id=1, source_target_pairs={{0,1},{1,2},{2,3},{3,4},{4,5},{5,6},{6,7},{7,8},{8,9},{9,10},{10,1... | collective-permute-start | bytes 1572872 | tf_op jit(solution)/shard_map/ppermute | solution.py:29
  30.5 0.7 copy-start.6
  30.5 0.7 copy-start.12
  31.2 12.5 %copy-start.1 = (bf16[1,128,2048]{2,1,0:T(8,128)(2,1)S(1)}, bf16[1,128,2048]{2,1,0:T(8,128)(2,1)}, u32[]{:S(2)}) copy-start(bf16[1,128,2048]{2,1,0:T(8,128)(2,1)} %k_ref.5) | copy-start | bytes 1572868
  31.2 12.6 %copy-start.8 = (bf16[1,128,2048]{2,1,0:T(8,128)(2,1)S(1)}, bf16[1,128,2048]{2,1,0:T(8,128)(2,1)}, u32[]{:S(2)}) copy-start(bf16[1,128,2048]{2,1,0:T(8,128)(2,1)} %q_ref.5) | copy-start | bytes 1572868
  34.4 41.6 %collective-permute-start.5 = (bf16[1,256,2048]{2,1,0:T(8,128)(2,1)S(1)}, bf16[1,256,2048]{2,1,0:T(8,128)(2,1)S(1)}, u32[]{:S(2)}, u32[]{:S(2)}) collective-permute-start(bf16[1,256,2048]{2,1,0:T(8,128)(2,1)S(1)} %get-tuple-element.33.n_ref.n0_ref.d0_ref), channel_id=1, source_target_pairs={{0,1},{1,2},{2,3},{3,4},{4,5},{5,6},{6,7},{7,8},{8,9},{9,10},{10,1... | collective-permute-start | bytes 3145736 | tf_op jit(solution)/shard_map/ppermute | solution.py:29
  36.4 39.7 %collective-permute-start.4 = (bf16[1,256,2048]{2,1,0:T(8,128)(2,1)S(1)}, bf16[1,256,2048]{2,1,0:T(8,128)(2,1)S(1)}, u32[]{:S(2)}, u32[]{:S(2)}) collective-permute-start(bf16[1,256,2048]{2,1,0:T(8,128)(2,1)S(1)} %get-tuple-element.33.n_ref.n0_ref.d0_ref), channel_id=1, source_target_pairs={{0,63},{1,0},{2,1},{3,2},{4,3},{5,4},{6,5},{7,6},{8,7},{9,8},{10,9... | collective-permute-start | bytes 3145736 | tf_op jit(solution)/shard_map/ppermute | solution.py:29
  61.0 11.0 %all-to-all-start.1 = ((f32[8,16,128]{2,1,0:T(8,128)}), f32[8,16,128]{2,1,0:T(8,128)S(1)}, u32[]{:S(2)}, u32[]{:S(2)}) async-start(f32[8,16,128]{2,1,0:T(8,128)} %broadcast_in_dim.4), calls=%async_computation.1 | async-start | bytes 131072 | tf_op jit(solution)/shard_map/all_to_all | solution.py:162
  64.8 11.3 %collective-permute-start.7 = (f32[64,128]{1,0:T(8,128)S(1)}, f32[64,128]{1,0:T(8,128)S(1)}, u32[]{:S(2)}, u32[]{:S(2)}) collective-permute-start(f32[64,128]{1,0:T(8,128)S(1)} %get-tuple-element.36.s0_ref), channel_id=1, source_target_pairs={{0,63},{1,0},{2,1},{3,2},{4,3},{5,4},{6,5},{7,6},{8,7},{9,8},{10,9... | collective-permute-start | bytes 98312 | tf_op jit(solution)/shard_map/ppermute | solution.py:29
  68.9 8.0 %collective-permute-start.6 = (f32[64,128]{1,0:T(8,128)S(1)}, f32[64,128]{1,0:T(8,128)S(1)}, u32[]{:S(2)}, u32[]{:S(2)}) collective-permute-start(f32[64,128]{1,0:T(8,128)S(1)} %get-tuple-element.36.s0_ref), channel_id=1, source_target_pairs={{0,1},{1,2},{2,3},{3,4},{4,5},{5,6},{6,7},{7,8},{8,9},{9,10},{10,1... | collective-permute-start | bytes 98312 | tf_op jit(solution)/shard_map/ppermute | solution.py:29
  72.7 10.9 %all-to-all-start.2 = ((f32[8,16,128]{2,1,0:T(8,128)}), f32[8,16,128]{2,1,0:T(8,128)S(1)}, u32[]{:S(2)}, u32[]{:S(2)}) async-start(f32[8,16,128]{2,1,0:T(8,128)} %broadcast_in_dim.5), calls=%async_computation.2 | async-start | bytes 131072 | tf_op jit(solution)/shard_map/all_to_all | solution.py:299
  76.9 1.0 %copy-start.2 = (bf16[1,128,2048]{2,1,0:T(8,128)(2,1)S(1)}, bf16[1,128,2048]{2,1,0:T(8,128)(2,1)}, u32[]{:S(2)}) copy-start(bf16[1,128,2048]{2,1,0:T(8,128)(2,1)} %k_ref.5) | copy-start | bytes 1572868
  77.9 1.0 %copy-start.5 = (bf16[1,128,2048]{2,1,0:T(8,128)(2,1)S(1)}, bf16[1,128,2048]{2,1,0:T(8,128)(2,1)}, u32[]{:S(2)}) copy-start(bf16[1,128,2048]{2,1,0:T(8,128)(2,1)} %v_ref.5) | copy-start | bytes 1572868

commit v4 on v3

--- a/solution.py
+++ b/solution.py
@@ -50,7 +50,7 @@
     out_ref[0, 2 * strip :, :] = valid.astype(jnp.float32).astype(jnp.bfloat16)
 
 
-def prep_kernel(k_ref, v_ref, q_ref, do_ref, gain_ref, kv_ref, nd_ref):
+def prep_kernel(k_ref, v_ref, k_all_ref, v_all_ref, q_ref, do_ref, gain_ref, kv_ref, nd_ref, own_ref):
     step = pl.program_id(0)
     strip = k_ref.shape[1]
     kv_ref[0, :strip, :] = k_ref[0]
@@ -62,6 +62,8 @@
         scale = lax.rsqrt(jnp.mean(q * q, axis=-1, keepdims=True) + EPS)
         nd_ref[0, :strip, columns_of(i)] = (q * scale * gain).astype(jnp.bfloat16)
     nd_ref[0, strip:, :] = do_ref[0]
+    own_ref[0, :strip, :] = k_all_ref[0]
+    own_ref[0, strip:, :] = v_all_ref[0]
 
 
 def query_kernel(
@@ -222,20 +224,22 @@
     )(own_bounds, keys, values)
     kv0_left, kv0_right = shifted(kv0, "view", 1), shifted(kv0, "view", -1)
     late = block(0, early_width // slim, slim)
-    kv1, nd = call(
+    kv1, nd, kv_own = call(
         prep_kernel,
         parts,
-        [late, late, block(0, 0, part), block(0, 0, part), whole],
+        [late, late] + [block(0, 0, part)] * 4 + [whole],
         [
             pl.BlockSpec((1, 2 * strip, slim), lambda i: (0, 0, i)),
+            pl.BlockSpec((1, 2 * strip, part), lambda i: (0, 0, i)),
             pl.BlockSpec((1, 2 * strip, part), lambda i: (0, 0, i)),
         ],
         [
             jax.ShapeDtypeStruct((1, 2 * strip, late_width), jnp.bfloat16),
             jax.ShapeDtypeStruct((1, 2 * strip, width), jnp.bfloat16),
+            jax.ShapeDtypeStruct((1, 2 * strip, width), jnp.bfloat16),
         ],
         cost=140,
-    )(keys, values, queries, out_grad, gain)
+    )(keys, values, keys, values, queries, out_grad, gain)
 
     kv1_left, kv1_right = shifted(kv1, "view", 1), shifted(kv1, "view", -1)
 
@@ -289,12 +293,12 @@
     kgrad, vgrad = call(
         key_kernel,
         steps // 2,
-        [scalars] + [block(0, 0, both)] * 2 + own * 3 + [stat_block] * 3,
+        [scalars] + own * 4 + [stat_block] * 3,
         [block(0, 0, both)] * 2,
         [wide, wide],
         cost=30,
     )(
-        own_bounds, keys, values, nd, nd, nd_left, nd_left, nd_right, nd_right, stats, s_left, s_right
+        own_bounds, kv_own, kv_own, nd, nd, nd_left, nd_left, nd_right, nd_right, stats, s_left, s_right
     )
     blocks = lax.all_to_all(copies(gain_grad, ring), "view", 0, 0, axis_index_groups=along, tiled=True)
     gain_grad = jnp.sum(tied(blocks, kgrad), axis=0)

time: 85.2 us -> 85.3 us (level)
  local copies, waits for them, and re-layouts: 7.14 us -> 5.08 us
  waiting for transfers between devices: 4.4 us -> 5.67 us
    unnamed x26 -> x22, local copies, waits for them, and re-layouts: 5.89 us -> 3.81 us
    all_to_all x1, waiting for transfers between devices: 0.01 us -> 1.51 us  [on_device(): lax.all_to_all(copies(gain_grad, ring), 'view', 0, 0, axis_index_groups=a...]
  transfers between devices with their start and end apart: 10 -> 10, of which waited for: 4 -> 5; matrix products, arithmetic and copies ran while one was open for 2% -> 2% of each run, Pallas kernels for 14% -> 15%
where the time goes in v4:
time: 85.3 us; the launch traced here: 84.1 us
  starting transfers between devices  43.9 us (51%)
  Pallas kernels  14.5 us (17%)
  blocking collectives  13.5 us (16%)
  waiting for transfers between devices  5.67 us (7%)
  local copies, waits for them, and re-layouts  5.08 us (6%)
    ppermute x8, starting transfers between devices, shifted(): lax.ppermute(array, axis, [(i, (i + by) % count) for i in range(count)])  36.7 us
    pallas_call x5, Pallas kernels, call(): run(*(pltpu.with_memory_space_constraint(a, pltpu.VMEM) if kernel is key_...  14.5 us
    all_to_all x1, blocking collectives, total_over(): lax.all_to_all(blocks, axis, 0, 0, axis_index_groups=groups, tiled=True)  13.5 us
    all_to_all x1, starting transfers between devices, total_over(): lax.all_to_all(blocks, axis, 0, 0, axis_index_groups=groups, tiled=True)  3.81 us
    unnamed x22, local copies, waits for them, and re-layouts  3.81 us
    all_to_all x1, starting transfers between devices, on_device(): lax.all_to_all(copies(gain_grad, ring), 'view', 0, 0, axis_index_groups=a...  3.35 us
    ppermute x8, waiting for transfers between devices, shifted(): lax.ppermute(array, axis, [(i, (i + by) % count) for i in range(count)])  2.85 us
  transfers between devices with their start and end apart: 10, of which 5 were waited for; matrix products, arithmetic and copies ran while one was open for 2% of the time, Pallas kernels for 15%

profile of v4, /device:TPU:1, one launch (start us, length us, event | category | flops | bytes accessed | tf_op | source)
XLA Modules:
  0.0 84.1 jit_solution(14983707442833842999)
XLA Ops:
  0.7 1.9 %pack_kernel.1 = bf16[1,272,1024]{2,1,0:T(8,128)(2,1)} custom-call(s32[2]{0:T(128)} %bitcast.2, bf16[1,128,2048]{2,1,0:T(8,128)(2,1)} %k0_ref.3, bf16[1,128,2048]{2,1,0:T(8,128)(2,1)} %v0_ref.3), custom_call_target="tpu_custom_call" | custom-call | bytes 2097152 | tf_op jit(solution)/shard_map/pack_kernel/pallas_call | solution.py:211
  2.6 4.8 %collective-permute-start.2 = (bf16[1,272,1024]{2,1,0:T(8,128)(2,1)}, bf16[1,272,1024]{2,1,0:T(8,128)(2,1)S(1)}, u32[]{:S(2)}, u32[]{:S(2)}) collective-permute-start(bf16[1,272,1024]{2,1,0:T(8,128)(2,1)} %pack_kernel.1), channel_id=1, source_target_pairs={{0,1},{1,2},{2,3},{3,4},{4,5},{5,6},{6,7},{7,8},{8,9},{9,10},{10,1... | collective-permute-start | bytes 1671176 | tf_op jit(solution)/shard_map/ppermute | solution.py:29
  7.4 11.5 %collective-permute-start.1 = (bf16[1,272,1024]{2,1,0:T(8,128)(2,1)}, bf16[1,272,1024]{2,1,0:T(8,128)(2,1)S(1)}, u32[]{:S(2)}, u32[]{:S(2)}) collective-permute-start(bf16[1,272,1024]{2,1,0:T(8,128)(2,1)} %pack_kernel.1), channel_id=1, source_target_pairs={{0,63},{1,0},{2,1},{3,2},{4,3},{5,4},{6,5},{7,6},{8,7},{9,8},{10,9... | collective-permute-start | bytes 1671176 | tf_op jit(solution)/shard_map/ppermute | solution.py:29
  18.9 1.0 %copy-done.2 = bf16[1,128,2048]{2,1,0:T(8,128)(2,1)S(1)} copy-done((bf16[1,128,2048]{2,1,0:T(8,128)(2,1)S(1)}, bf16[1,128,2048]{2,1,0:T(8,128)(2,1)}, u32[]{:S(2)}) %copy-start.2) | copy-done | bytes 524312
  20.0 1.0 %copy-done.5 = bf16[1,128,2048]{2,1,0:T(8,128)(2,1)S(1)} copy-done((bf16[1,128,2048]{2,1,0:T(8,128)(2,1)S(1)}, bf16[1,128,2048]{2,1,0:T(8,128)(2,1)}, u32[]{:S(2)}) %copy-start.5) | copy-done | bytes 524312
  21.0 1.0 %copy-done.7 = bf16[1,128,2048]{2,1,0:T(8,128)(2,1)S(1)} copy-done((bf16[1,128,2048]{2,1,0:T(8,128)(2,1)S(1)}, bf16[1,128,2048]{2,1,0:T(8,128)(2,1)}, u32[]{:S(2)}) %copy-start.7) | copy-done | bytes 524312
  22.1 1.0 %prep_kernel.1 = (bf16[1,256,1024]{2,1,0:T(8,128)(2,1)S(1)}, bf16[1,256,2048]{2,1,0:T(8,128)(2,1)S(1)}, bf16[1,256,2048]{2,1,0:T(8,128)(2,1)S(1)}) custom-call(bf16[1,128,2048]{2,1,0:T(8,128)(2,1)S(1)} %copy-done, bf16[1,128,2048]{2,1,0:T(8,128)(2,1)S(1)} %copy-done.2, bf16[1,128,2048]{2,1,0:T(8,128)(2,1)S(1)} %copy-done, ...), custom_call_target="tpu_custom_call" | custom-call | flops 4697620480 | bytes 2097152 | tf_op jit(solution)/shard_map/prep_kernel/pallas_call | solution.py:211
  23.1 3.4 %collective-permute-start.3 = (bf16[1,256,1024]{2,1,0:T(8,128)(2,1)S(1)}, bf16[1,256,1024]{2,1,0:T(8,128)(2,1)S(1)}, u32[]{:S(2)}, u32[]{:S(2)}) collective-permute-start(bf16[1,256,1024]{2,1,0:T(8,128)(2,1)S(1)} %get-tuple-element.25), channel_id=1, source_target_pairs={{0,63},{1,0},{2,1},{3,2},{4,3},{5,4},{6,5},{7,6},{8,7},{9,8},{10,9... | collective-permute-start | bytes 1572872 | tf_op jit(solution)/shard_map/ppermute | solution.py:29
  26.4 1.9 %collective-permute-start = (bf16[1,256,1024]{2,1,0:T(8,128)(2,1)S(1)}, bf16[1,256,1024]{2,1,0:T(8,128)(2,1)S(1)}, u32[]{:S(2)}, u32[]{:S(2)}) collective-permute-start(bf16[1,256,1024]{2,1,0:T(8,128)(2,1)S(1)} %get-tuple-element.25), channel_id=1, source_target_pairs={{0,1},{1,2},{2,3},{3,4},{4,5},{5,6},{6,7},{7,8},{8,9},{9,10},{10,1... | collective-permute-start | bytes 1572872 | tf_op jit(solution)/shard_map/ppermute | solution.py:29
  28.4 1.2 %collective-permute-done.2.k1_ref.v1_ref.m1_ref = bf16[1,272,1024]{2,1,0:T(8,128)(2,1)S(1)} collective-permute-done((bf16[1,272,1024]{2,1,0:T(8,128)(2,1)}, bf16[1,272,1024]{2,1,0:T(8,128)(2,1)S(1)}, u32[]{:S(2)}, u32[]{:S(2)}) %collective-permute-start.2) | collective-permute-done | bytes 557088 | tf_op jit(solution)/shard_map/ppermute | solution.py:29
  29.5 1.0 %collective-permute-done.1.k2_ref.v2_ref.m2_ref = bf16[1,272,1024]{2,1,0:T(8,128)(2,1)S(1)} collective-permute-done((bf16[1,272,1024]{2,1,0:T(8,128)(2,1)}, bf16[1,272,1024]{2,1,0:T(8,128)(2,1)S(1)}, u32[]{:S(2)}, u32[]{:S(2)}) %collective-permute-start.1) | collective-permute-done | bytes 557088 | tf_op jit(solution)/shard_map/ppermute | solution.py:29
  31.2 3.3 %query_kernel.2 = (bf16[1,128,2048]{2,1,0:T(8,128)(2,1)}, bf16[1,128,2048]{2,1,0:T(8,128)(2,1)}, f32[64,128]{1,0:T(8,128)S(1)}, f32[1,8,128]{2,1,0:T(8,128)S(1)}) custom-call(s32[2]{0:T(128)S(1)} %bitcast.6, s32[2]{0:T(128)S(1)} %bitcast.3, bf16[1,128,2048]{2,1,0:T(8,128)(2,1)S(1)} %copy-done.5, ...), custom_call_target="tpu_custom_call" | custom-call | flops 100663296000 | bytes 2097152 | tf_op jit(solution)/shard_map/query_kernel/pallas_call | solution.py:211
  34.5 1.9 %collective-permute-start.5 = (bf16[1,256,2048]{2,1,0:T(8,128)(2,1)S(1)}, bf16[1,256,2048]{2,1,0:T(8,128)(2,1)S(1)}, u32[]{:S(2)}, u32[]{:S(2)}) collective-permute-start(bf16[1,256,2048]{2,1,0:T(8,128)(2,1)S(1)} %get-tuple-element.35.n_ref.n0_ref.d0_ref), channel_id=1, source_target_pairs={{0,1},{1,2},{2,3},{3,4},{4,5},{5,6},{6,7},{7,8},{8,9},{9,10},{10,1... | collective-permute-start | bytes 3145736 | tf_op jit(solution)/shard_map/ppermute | solution.py:29
  36.4 7.3 %collective-permute-start.4 = (bf16[1,256,2048]{2,1,0:T(8,128)(2,1)S(1)}, bf16[1,256,2048]{2,1,0:T(8,128)(2,1)}, u32[]{:S(2)}, u32[]{:S(2)}) collective-permute-start(bf16[1,256,2048]{2,1,0:T(8,128)(2,1)S(1)} %get-tuple-element.35.n_ref.n0_ref.d0_ref), channel_id=1, source_target_pairs={{0,63},{1,0},{2,1},{3,2},{4,3},{5,4},{6,5},{7,6},{8,7},{9,8},{10,9... | collective-permute-start | bytes 3145736 | tf_op jit(solution)/shard_map/ppermute | solution.py:29
  43.7 3.3 %query_kernel.3 = (bf16[1,128,2048]{2,1,0:T(8,128)(2,1)}, bf16[1,128,2048]{2,1,0:T(8,128)(2,1)}, f32[64,128]{1,0:T(8,128)S(1)}, f32[8,16,128]{2,1,0:T(8,128)S(1)}) custom-call(s32[2]{0:T(128)S(1)} %bitcast.7, s32[2]{0:T(128)S(1)} %bitcast.4, bf16[1,128,2048]{2,1,0:T(8,128)(2,1)S(1)} %copy-done.6, ...), custom_call_target="tpu_custom_call", output_to_operand_aliasing={{0}: (14, {}), {1}: (15, {}), {2}: (16, {})} | custom-call | flops 100663296000 | bytes 2097152 | tf_op jit(solution)/shard_map/query_kernel/pallas_call | solution.py:211
  47.1 13.5 %all_to_all.15 = f32[8,16,128]{2,1,0:T(8,128)S(1)} all-to-all(f32[8,16,128]{2,1,0:T(8,128)S(1)} %get-tuple-element.41), channel_id=1, replica_groups=mesh['dp'=8,'view'=64] {'dp'}, dimensions={0} | all-to-all | bytes 131072 | tf_op jit(solution)/shard_map/all_to_all | solution.py:164
  61.2 3.8 %all-to-all-start.1 = ((f32[8,16,128]{2,1,0:T(8,128)}), f32[8,16,128]{2,1,0:T(8,128)S(1)}, u32[]{:S(2)}, u32[]{:S(2)}) async-start(f32[8,16,128]{2,1,0:T(8,128)} %broadcast_in_dim.4), calls=%async_computation.1 | async-start | bytes 131072 | tf_op jit(solution)/shard_map/all_to_all | solution.py:164
  65.0 4.0 %collective-permute-start.7 = (f32[64,128]{1,0:T(8,128)S(1)}, f32[64,128]{1,0:T(8,128)S(1)}, u32[]{:S(2)}, u32[]{:S(2)}) collective-permute-start(f32[64,128]{1,0:T(8,128)S(1)} %get-tuple-element.38.s0_ref), channel_id=1, source_target_pairs={{0,63},{1,0},{2,1},{3,2},{4,3},{5,4},{6,5},{7,6},{8,7},{9,8},{10,9... | collective-permute-start | bytes 98312 | tf_op jit(solution)/shard_map/ppermute | solution.py:29
  69.0 1.9 %collective-permute-start.6 = (f32[64,128]{1,0:T(8,128)S(1)}, f32[64,128]{1,0:T(8,128)S(1)}, u32[]{:S(2)}, u32[]{:S(2)}) collective-permute-start(f32[64,128]{1,0:T(8,128)S(1)} %get-tuple-element.38.s0_ref), channel_id=1, source_target_pairs={{0,1},{1,2},{2,3},{3,4},{4,5},{5,6},{6,7},{7,8},{8,9},{9,10},{10,1... | collective-permute-start | bytes 98312 | tf_op jit(solution)/shard_map/ppermute | solution.py:29
  70.9 1.3 %all-to-all-done.1 = f32[8,16,128]{2,1,0:T(8,128)S(1)} async-done(((f32[8,16,128]{2,1,0:T(8,128)}), f32[8,16,128]{2,1,0:T(8,128)S(1)}, u32[]{:S(2)}, u32[]{:S(2)}) %all-to-all-start.1) | async-done | bytes 65568 | tf_op jit(solution)/shard_map/all_to_all | solution.py:164
  72.9 3.3 %all-to-all-start.2 = ((f32[8,16,128]{2,1,0:T(8,128)}), f32[8,16,128]{2,1,0:T(8,128)S(1)}, u32[]{:S(2)}, u32[]{:S(2)}) async-start(f32[8,16,128]{2,1,0:T(8,128)} %broadcast_in_dim.5), calls=%async_computation.2 | async-start | bytes 131072 | tf_op jit(solution)/shard_map/all_to_all | solution.py:303
  76.3 0.7 collective-permute-done.6.s1_ref
  77.0 5.0 %key_kernel.1 = (bf16[1,128,2048]{2,1,0:T(8,128)(2,1)}, bf16[1,128,2048]{2,1,0:T(8,128)(2,1)}) custom-call(s32[2]{0:T(128)S(1)} %bitcast.5, bf16[1,256,2048]{2,1,0:T(8,128)(2,1)S(1)} %get-tuple-element.34.k_ref.v_ref, bf16[1,256,2048]{2,1,0:T(8,128)(2,1)S(1)} %get-tuple-element.34.k_ref.v_ref, ...), custom_call_target="tpu_custom_call" | custom-call | flops 1006632960 | bytes 2097152 | tf_op jit(solution)/shard_map/key_kernel/pallas_call | solution.py:211
  82.0 1.5 %all-to-all-done.2 = f32[8,16,128]{2,1,0:T(8,128)S(1)} async-done(((f32[8,16,128]{2,1,0:T(8,128)}), f32[8,16,128]{2,1,0:T(8,128)S(1)}, u32[]{:S(2)}, u32[]{:S(2)}) %all-to-all-start.2) | async-done | bytes 65568 | tf_op jit(solution)/shard_map/all_to_all | solution.py:303
  (29 shorter events, 2.6 us)
Async XLA Ops:
  0.6 18.3 %copy-start = (bf16[1,128,2048]{2,1,0:T(8,128)(2,1)S(1)}, bf16[1,128,2048]{2,1,0:T(8,128)(2,1)}, u32[]{:S(2)}) copy-start(bf16[1,128,2048]{2,1,0:T(8,128)(2,1)} %k0_ref.3) | copy-start | bytes 1572868
  0.6 18.3 %copy-start.9 = (f32[16,128]{1,0:T(8,128)S(1)}, f32[16,128]{1,0:T(8,128)}, u32[]{:S(2)}) copy-start(f32[16,128]{1,0:T(8,128)} %gain_ref.5) | copy-start | bytes 24580
  2.6 26.9 %collective-permute-start.2 = (bf16[1,272,1024]{2,1,0:T(8,128)(2,1)}, bf16[1,272,1024]{2,1,0:T(8,128)(2,1)S(1)}, u32[]{:S(2)}, u32[]{:S(2)}) collective-permute-start(bf16[1,272,1024]{2,1,0:T(8,128)(2,1)} %pack_kernel.1), channel_id=1, source_target_pairs={{0,1},{1,2},{2,3},{3,4},{4,5},{5,6},{6,7},{7,8},{8,9},{9,10},{10,1... | collective-permute-start | bytes 1671176 | tf_op jit(solution)/shard_map/ppermute | solution.py:29
  7.4 23.1 %collective-permute-start.1 = (bf16[1,272,1024]{2,1,0:T(8,128)(2,1)}, bf16[1,272,1024]{2,1,0:T(8,128)(2,1)S(1)}, u32[]{:S(2)}, u32[]{:S(2)}) collective-permute-start(bf16[1,272,1024]{2,1,0:T(8,128)(2,1)} %pack_kernel.1), channel_id=1, source_target_pairs={{0,63},{1,0},{2,1},{3,2},{4,3},{5,4},{6,5},{7,6},{8,7},{9,8},{10,9... | collective-permute-start | bytes 1671176 | tf_op jit(solution)/shard_map/ppermute | solution.py:29
  18.9 1.0 %copy-start.2 = (bf16[1,128,2048]{2,1,0:T(8,128)(2,1)S(1)}, bf16[1,128,2048]{2,1,0:T(8,128)(2,1)}, u32[]{:S(2)}) copy-start(bf16[1,128,2048]{2,1,0:T(8,128)(2,1)} %v0_ref.3) | copy-start | bytes 1572868
  20.0 1.0 %copy-start.5 = (bf16[1,128,2048]{2,1,0:T(8,128)(2,1)S(1)}, bf16[1,128,2048]{2,1,0:T(8,128)(2,1)}, u32[]{:S(2)}) copy-start(bf16[1,128,2048]{2,1,0:T(8,128)(2,1)} %q_ref.5) | copy-start | bytes 1572868
  21.0 1.0 %copy-start.7 = (bf16[1,128,2048]{2,1,0:T(8,128)(2,1)S(1)}, bf16[1,128,2048]{2,1,0:T(8,128)(2,1)}, u32[]{:S(2)}) copy-start(bf16[1,128,2048]{2,1,0:T(8,128)(2,1)} %do_ref.5) | copy-start | bytes 1572868
  22.1 8.4 %copy-start.3 = (bf16[1,128,2048]{2,1,0:T(8,128)(2,1)S(1)}, bf16[1,128,2048]{2,1,0:T(8,128)(2,1)}, u32[]{:S(2)}) copy-start(bf16[1,128,2048]{2,1,0:T(8,128)(2,1)} %v0_ref.3) | copy-start | bytes 1572868
  22.1 8.4 %copy-start.8 = (bf16[1,128,2048]{2,1,0:T(8,128)(2,1)S(1)}, bf16[1,128,2048]{2,1,0:T(8,128)(2,1)}, u32[]{:S(2)}) copy-start(bf16[1,128,2048]{2,1,0:T(8,128)(2,1)} %do_ref.5) | copy-start | bytes 1572868
  23.1 20.6 %collective-permute-start.3 = (bf16[1,256,1024]{2,1,0:T(8,128)(2,1)S(1)}, bf16[1,256,1024]{2,1,0:T(8,128)(2,1)S(1)}, u32[]{:S(2)}, u32[]{:S(2)}) collective-permute-start(bf16[1,256,1024]{2,1,0:T(8,128)(2,1)S(1)} %get-tuple-element.25), channel_id=1, source_target_pairs={{0,63},{1,0},{2,1},{3,2},{4,3},{5,4},{6,5},{7,6},{8,7},{9,8},{10,9... | collective-permute-start | bytes 1572872 | tf_op jit(solution)/shard_map/ppermute | solution.py:29
  26.4 17.3 %collective-permute-start = (bf16[1,256,1024]{2,1,0:T(8,128)(2,1)S(1)}, bf16[1,256,1024]{2,1,0:T(8,128)(2,1)S(1)}, u32[]{:S(2)}, u32[]{:S(2)}) collective-permute-start(bf16[1,256,1024]{2,1,0:T(8,128)(2,1)S(1)} %get-tuple-element.25), channel_id=1, source_target_pairs={{0,1},{1,2},{2,3},{3,4},{4,5},{5,6},{6,7},{7,8},{8,9},{9,10},{10,1... | collective-permute-start | bytes 1572872 | tf_op jit(solution)/shard_map/ppermute | solution.py:29
  30.5 0.7 copy-start.4
  30.5 0.7 copy-start.10
  31.2 12.5 %copy-start.1 = (bf16[1,128,2048]{2,1,0:T(8,128)(2,1)S(1)}, bf16[1,128,2048]{2,1,0:T(8,128)(2,1)}, u32[]{:S(2)}) copy-start(bf16[1,128,2048]{2,1,0:T(8,128)(2,1)} %k0_ref.3) | copy-start | bytes 1572868
  31.2 12.6 %copy-start.6 = (bf16[1,128,2048]{2,1,0:T(8,128)(2,1)S(1)}, bf16[1,128,2048]{2,1,0:T(8,128)(2,1)}, u32[]{:S(2)}) copy-start(bf16[1,128,2048]{2,1,0:T(8,128)(2,1)} %q_ref.5) | copy-start | bytes 1572868
  34.5 41.8 %collective-permute-start.5 = (bf16[1,256,2048]{2,1,0:T(8,128)(2,1)S(1)}, bf16[1,256,2048]{2,1,0:T(8,128)(2,1)S(1)}, u32[]{:S(2)}, u32[]{:S(2)}) collective-permute-start(bf16[1,256,2048]{2,1,0:T(8,128)(2,1)S(1)} %get-tuple-element.35.n_ref.n0_ref.d0_ref), channel_id=1, source_target_pairs={{0,1},{1,2},{2,3},{3,4},{4,5},{5,6},{6,7},{7,8},{8,9},{9,10},{10,1... | collective-permute-start | bytes 3145736 | tf_op jit(solution)/shard_map/ppermute | solution.py:29
  36.4 39.9 %collective-permute-start.4 = (bf16[1,256,2048]{2,1,0:T(8,128)(2,1)S(1)}, bf16[1,256,2048]{2,1,0:T(8,128)(2,1)}, u32[]{:S(2)}, u32[]{:S(2)}) collective-permute-start(bf16[1,256,2048]{2,1,0:T(8,128)(2,1)S(1)} %get-tuple-element.35.n_ref.n0_ref.d0_ref), channel_id=1, source_target_pairs={{0,63},{1,0},{2,1},{3,2},{4,3},{5,4},{6,5},{7,6},{8,7},{9,8},{10,9... | collective-permute-start | bytes 3145736 | tf_op jit(solution)/shard_map/ppermute | solution.py:29
  61.2 11.0 %all-to-all-start.1 = ((f32[8,16,128]{2,1,0:T(8,128)}), f32[8,16,128]{2,1,0:T(8,128)S(1)}, u32[]{:S(2)}, u32[]{:S(2)}) async-start(f32[8,16,128]{2,1,0:T(8,128)} %broadcast_in_dim.4), calls=%async_computation.1 | async-start | bytes 131072 | tf_op jit(solution)/shard_map/all_to_all | solution.py:164
  65.0 11.3 %collective-permute-start.7 = (f32[64,128]{1,0:T(8,128)S(1)}, f32[64,128]{1,0:T(8,128)S(1)}, u32[]{:S(2)}, u32[]{:S(2)}) collective-permute-start(f32[64,128]{1,0:T(8,128)S(1)} %get-tuple-element.38.s0_ref), channel_id=1, source_target_pairs={{0,63},{1,0},{2,1},{3,2},{4,3},{5,4},{6,5},{7,6},{8,7},{9,8},{10,9... | collective-permute-start | bytes 98312 | tf_op jit(solution)/shard_map/ppermute | solution.py:29
  69.0 8.0 %collective-permute-start.6 = (f32[64,128]{1,0:T(8,128)S(1)}, f32[64,128]{1,0:T(8,128)S(1)}, u32[]{:S(2)}, u32[]{:S(2)}) collective-permute-start(f32[64,128]{1,0:T(8,128)S(1)} %get-tuple-element.38.s0_ref), channel_id=1, source_target_pairs={{0,1},{1,2},{2,3},{3,4},{4,5},{5,6},{6,7},{7,8},{8,9},{9,10},{10,1... | collective-permute-start | bytes 98312 | tf_op jit(solution)/shard_map/ppermute | solution.py:29
  72.9 10.6 %all-to-all-start.2 = ((f32[8,16,128]{2,1,0:T(8,128)}), f32[8,16,128]{2,1,0:T(8,128)S(1)}, u32[]{:S(2)}, u32[]{:S(2)}) async-start(f32[8,16,128]{2,1,0:T(8,128)} %broadcast_in_dim.5), calls=%async_computation.2 | async-start | bytes 131072 | tf_op jit(solution)/shard_map/all_to_all | solution.py:303
